TPU v7x, 32 devices: a whole 2x2x4 slice. The times are simulated.
32 devices in a mesh: runs: 2 (over y), cuts: 4 (over z), event: 4 (over x, core).
Axes of the slice: x: 2, y: 2, z: 4, core: 2. Of those that a mesh axis runs over, the one named last changes fastest.
Arguments:
- partials: float32 [4, 2, 262144], P('event', None, ('runs', 'cuts')), parts along dimension 2
- coords: float32 [3, 262144], P(None, ('runs', 'cuts')), parts along dimension 1, may hold values from 0 to 800
- volume: float32 [262144], P(('runs', 'cuts')), parts along dimension 0, may hold values from 0.5 to 4
- send_blocks: int32 [8, 4, 4, 64], P(('runs', 'cuts'), 'event'), parts along dimension 0, may hold values from 0 to 255
- halo_counts: int32 [8, 4, 4], P(('runs', 'cuts'), 'event'), parts along dimension 0, may hold values from 16 to 64
- source_slots: int32 [8, 4, 64, 16], P(('runs', 'cuts'), 'event'), parts along dimension 0, may hold values from 0 to 511, as said below
- source_counts: int32 [8, 4, 64], P(('runs', 'cuts'), 'event'), parts along dimension 0, may hold values from 8 to 16
Outputs:
- smoothed: float32 [2, 262144], P(None, ('runs', 'cuts', 'event')), parts along dimension 1
There are 2 independent parts, one for each index of `runs`. A program takes and returns all parts, laid end to end along the dimension named above; each array names one. Nothing has to cross between parts.
Inputs may be any that keep to these rules, and one draw needn't show every extreme that they name: `source_slots`: slot 0 of target block t of owner (c, e) is its own block, e * 64 + t; every slot names a block of the own slice or a halo slot.
All inputs are finite; a program needn't handle non-finite values.
Results may differ from a plain program's by a relative error of at most 0.00019.
Values sent between devices are 32-bit elements; how exact they have to be, the bound alone decides.
No kernel may reach another device: no remote copies, remote signals or barrier semaphores. Data moves between devices by JAX's collectives and lax.ppermute only.
A program may use at most 64 MiB of HBM per device.

v0:
```python
import functools
import math

import jax
import jax.numpy as jnp
from jax import lax
from jax.experimental import pallas as pl
from jax.experimental.pallas import tpu as pltpu
from jax.sharding import PartitionSpec as P

BLOCK = 128
FEATURES = 48
STEP_BITS = 4
STEP = 1 << STEP_BITS
FIELD = 10
sigma_km = 50.0
centre_km = 400.0
scale = math.sqrt(math.log2(math.e)) / sigma_km

f32 = jnp.float32
bf16 = jnp.bfloat16
i32 = jnp.int32


def vmem():
    return pl.BlockSpec(memory_space=pltpu.VMEM)


def smem():
    return pl.BlockSpec(memory_space=pltpu.SMEM)


def held(*arrays):
    return [pltpu.with_memory_space_constraint(a, pltpu.VMEM) for a in arrays]


def far(*arrays):
    return [pltpu.with_memory_space_constraint(a, pltpu.HBM) for a in arrays]


def lasting(microseconds):
    flops = int(microseconds * 1.15e9)
    return pl.CostEstimate(flops=flops, bytes_accessed=1000000, transcendentals=0)


def params(mib):
    return pltpu.CompilerParams(vmem_limit_bytes=mib << 20)


def swapped(block, stride, turn):
    devices = lax.axis_size("cuts")
    step = [stride, -stride] if turn == 0 else [-stride, stride]
    route = [(i, (i + step[(i // stride) % 2]) % devices) for i in range(devices)]
    return lax.ppermute(block, "cuts", route)


def crossed(block, axis, bit):
    route = [(i ^ bit, i) for i in range(lax.axis_size(axis))]
    return lax.ppermute(block, axis, route)


def split(values):
    high = values.astype(bf16).astype(f32)
    rest = values - high
    middle = rest.astype(bf16).astype(f32)
    return high, middle, rest - middle


def feature_rows(offsets, fourth, fifth):
    row = lax.broadcasted_iota(i32, (8, BLOCK), 0)
    rows = jnp.where(row == 3, fourth, jnp.where(row == 4, fifth, 0.0))
    return jnp.where(row < 3, offsets, rows)


def place(coords_ref, pad_ref, slot, b):
    at = pl.ds(pl.multiple_of(b * BLOCK, BLOCK), BLOCK)
    pad_ref[slot, 0:3, :] = (coords_ref[:, at] - centre_km) * scale
    offsets = pad_ref[slot]
    return offsets, -0.5 * jnp.sum(offsets * offsets, axis=0, keepdims=True)


def target_features(offsets, norm):
    high, middle, low = split(feature_rows(offsets, 1.0, norm))
    return jnp.concatenate([high, middle, low, high, middle, high], axis=0).astype(bf16)


def own_features_kernel(
    event_ref, coords_ref, volume_ref, source_ref, target_ref, mark_ref, pad_ref, log_ref
):
    block_total = volume_ref.shape[0]
    own_blocks = target_ref.shape[0]
    slots = pad_ref.shape[0]
    pad_ref[...] = jnp.zeros(pad_ref.shape, f32)
    log_ref[...] = jnp.log2(volume_ref[...])

    def some_sources(n, _):
        for slot in range(slots):
            b = n * slots + slot
            offsets, norm = place(coords_ref, pad_ref, slot, b)
            high, middle, low = split(feature_rows(offsets, norm + log_ref[pl.ds(b, 1), :], 1.0))
            rows = jnp.concatenate([high, high, high, middle, middle, low], axis=0)
            source_ref[b] = rows.astype(bf16).T
        return 0

    def some_targets(n, _):
        for slot in range(slots):
            t = n * slots + slot
            block = event_ref[0] * own_blocks + t
            target_ref[t] = target_features(*place(coords_ref, pad_ref, slot, block))
        return 0

    lax.fori_loop(0, block_total // slots, some_sources, 0)
    lax.fori_loop(0, own_blocks // slots, some_targets, 0)
    column = lax.broadcasted_iota(i32, (BLOCK, FEATURES), 1)
    source_ref[block_total] = jnp.where(column == 3, -10000.0, 0.0).astype(bf16)
    mark_ref[...] = jnp.zeros(mark_ref.shape, f32)


def own_features(event, coords, volume, own_blocks):
    block_total = volume.shape[0]
    return pl.pallas_call(
        own_features_kernel,
        out_shape=(
            pltpu.VMEM((block_total + 1, BLOCK, FEATURES), bf16),
            pltpu.VMEM((own_blocks, FEATURES, BLOCK), bf16),
            jax.ShapeDtypeStruct((8, BLOCK), f32),
        ),
        in_specs=[smem(), vmem(), vmem()],
        out_specs=(vmem(),) * 3,
        scratch_shapes=[pltpu.VMEM((16, 8, BLOCK), f32), pltpu.VMEM((block_total, BLOCK), f32)],
        compiler_params=params(8),
        cost_estimate=lasting(4),
        name="own_features",
    )(event, *held(coords, volume))


def coded(target, first, second):
    return (target << (2 * FIELD)) + (second << FIELD) + first


def decoded(code):
    mask = (1 << FIELD) - 1
    return code >> (2 * FIELD), code & mask, (code >> FIELD) & mask


def prepare_kernel(
    strides, capacity, event_ref, cut_ref, halo_given, slot_given, count_given, coords_given,
    volume_given, mine_given, coords_ref, volume_ref, mine_ref, own_ref, *refs,
):
    parcels, rest = refs[: 2 * len(strides)], refs[2 * len(strides) :]
    halo_ref, slot_ref, count_ref, row_ref, list_ref, arrival = rest
    width, own_blocks = slot_ref.shape
    block_total = volume_ref.shape[0]
    sets = len(parcels) + 1
    brought = [
        (halo_given, halo_ref), (slot_given, slot_ref), (count_given, count_ref),
        (coords_given, coords_ref), (volume_given, volume_ref), (mine_given, mine_ref),
    ]
    half = mine_ref.shape[1]
    at = pl.ds(pl.multiple_of((event_ref[0] & 1) * half, half), half)
    brought[5] = (mine_given.at[:, at], mine_ref)
    brought = [
        pltpu.make_async_copy(given, ref, arrival.at[n]) for n, (given, ref) in enumerate(brought)
    ]
    for copy in brought:
        copy.start()
    for copy in brought[:3]:
        copy.wait()
    row_ref[...] = jnp.zeros(row_ref.shape, i32)
    row_ref[0:width, 0:own_blocks] = slot_ref[...]
    row_ref[width : width + 1, 0:own_blocks] = count_ref[...]
    shape = (width, BLOCK)
    slots = row_ref[0:width]
    used = lax.broadcasted_iota(i32, shape, 0) < row_ref[width : width + 1]
    halo = slots - block_total
    lives = [used & (halo < 0)]
    for stride, members in strides:
        both = []
        for directions in members:
            live = jnp.zeros(shape, i32)
            for k in directions:
                near = (halo >= k * capacity) & (halo - k * capacity < halo_ref[0, k])
                live = live + (near & (halo < (k + 1) * capacity)).astype(i32)
            both.append(live)
        odd = (cut_ref[0] // stride) % 2
        for first, second in (both[::-1], both):
            live = first * (1 - odd) + second * odd
            lives.append(used & (live > 0))
    rows = sets * width
    live = jnp.concatenate([l.astype(f32) for l in lives], axis=0).astype(bf16)
    near = lax.broadcasted_iota(i32, (rows, rows), 0)
    across = lax.broadcasted_iota(i32, (rows, rows), 1)
    alike = near // width == across // width
    above = (alike & (across < near)).astype(f32).astype(bf16)
    rank = jnp.dot(above, live, preferred_element_type=f32).astype(i32)
    count = jnp.dot(alike.astype(f32).astype(bf16), live, preferred_element_type=f32)
    twos = ((count.astype(i32) + 1) >> 1).astype(f32).astype(bf16)
    near = lax.broadcasted_iota(i32, (BLOCK, BLOCK), 0)
    across = lax.broadcasted_iota(i32, (BLOCK, BLOCK), 1)
    earlier = (near < across).astype(f32).astype(bf16)
    before = jnp.dot(twos, earlier, preferred_element_type=f32).astype(i32)
    total = jnp.dot(twos, jnp.ones((BLOCK, BLOCK), bf16), preferred_element_type=f32).astype(i32)
    place_of = before + (rank >> 1)
    list_rows = own_blocks * width // (2 * BLOCK)
    high = jnp.full(shape, -1, i32)
    low = jnp.zeros(shape, i32)
    odd = jnp.zeros(shape, i32)
    for s in range(sets):
        part = slice(s * width, (s + 1) * width)
        high = jnp.where(lives[s], (place_of[part] >> 7) + s * list_rows, high)
        low = jnp.where(lives[s], place_of[part] & (BLOCK - 1), low)
        odd = jnp.where(lives[s], rank[part] & 1, odd)
    block = jnp.where(halo < 0, slots, halo) + 1
    even = 1 - odd
    target = lax.broadcasted_iota(i32, shape, 1)
    parts = [target * even, (block >> 3) * even, (block & 7) * even]
    parts = [p.astype(f32) for p in parts + [(block >> 3) * odd, (block & 7) * odd]]
    size = (sets * list_rows + 7) // 8 * 8
    list_row = lax.broadcasted_iota(i32, (size, BLOCK), 0)
    list_lane = lax.broadcasted_iota(i32, (BLOCK, BLOCK), 0)
    codes, places = [], []
    for i in range(width):
        hit = list_row == high[i : i + 1, :]
        codes.append(
            jnp.concatenate([jnp.where(hit, p[i : i + 1, :], 0.0) for p in parts], axis=0)
        )
        places.append((list_lane == low[i : i + 1, :]).astype(f32).astype(bf16))
    codes = jnp.concatenate([c.astype(bf16) for c in codes], axis=1)
    places = jnp.concatenate(places, axis=1)
    found = lax.dot_general(
        codes, places, (((1,), (1,)), ((), ())), preferred_element_type=f32
    ).astype(i32)
    target, *found = [found[n * size : (n + 1) * size] for n in range(5)]
    blocks = [found[0] * 8 + found[1] - 1, found[2] * 8 + found[3] - 1]
    for s in range(sets):
        part = slice(s * list_rows, (s + 1) * list_rows)
        spare = block_total if s == 0 else 4 * capacity
        pair = [jnp.where(b[part] < 0, spare, b[part]) for b in blocks]
        steps = jnp.maximum((total[s * width : s * width + 4] + STEP - 1) >> STEP_BITS, 1)
        if s == 0:
            list_ref[0, 0:list_rows] = coded(target[part], *pair)
            list_ref[0, list_rows:] = steps
        else:
            given = [*pair, target[part], steps]
            for n, values in enumerate(given):
                at = 3 * own_blocks + n * list_rows
                parcels[s - 1][at : at + list_rows] = values.astype(f32)
    sent = pltpu.make_async_copy(list_ref, own_ref, arrival.at[6])
    sent.start()
    for copy in brought[3:]:
        copy.wait()

    def some_coords(t, _):
        at = pl.multiple_of((event_ref[0] * own_blocks + t) * BLOCK, BLOCK)
        given = coords_ref[:, pl.ds(at, BLOCK)]
        for parcel in parcels:
            for r in range(3):
                parcel[pl.ds(r * own_blocks + t, 1), :] = given[r : r + 1]
        return 0

    lax.fori_loop(0, own_blocks, some_coords, 0, unroll=8)
    sent.wait()


def prepare(strides, capacity, event, cut, halo_counts, slots, counts, coords, volume, mine):
    width, own_blocks = slots.shape
    list_rows = own_blocks * width // (2 * BLOCK)
    parcel = jax.ShapeDtypeStruct((3 * own_blocks + 4 * list_rows, BLOCK), f32)
    return pl.pallas_call(
        functools.partial(prepare_kernel, strides, capacity),
        out_shape=(
            pltpu.VMEM(coords.shape, f32),
            pltpu.VMEM(volume.shape, f32),
            pltpu.VMEM((2, mine.shape[1] // 2), f32),
            pltpu.SMEM((1, list_rows + 4, BLOCK), i32),
        )
        + (parcel,) * (2 * len(strides)),
        in_specs=[smem()] * 2 + [pl.BlockSpec(memory_space=pltpu.HBM)] * 6,
        out_specs=(vmem(), vmem(), vmem(), smem()) + (vmem(),) * (2 * len(strides)),
        scratch_shapes=[
            pltpu.SMEM(halo_counts.shape, i32),
            pltpu.VMEM(slots.shape, i32),
            pltpu.VMEM(counts.shape, i32),
            pltpu.VMEM((width + 8, BLOCK), i32),
            pltpu.VMEM((1, list_rows + 4, BLOCK), i32),
            pltpu.SemaphoreType.DMA((7,)),
        ],
        compiler_params=params(8),
        cost_estimate=lasting(2),
        name="prepare",
    )(event, cut, *far(halo_counts, slots, counts, coords, volume, mine))


def halo_features_kernel(block_total, own_blocks, sent_ref, *refs):
    *given, target_ref, smem_ref, list_ref, pad_ref, row_ref, arrival = refs
    slots = pad_ref.shape[0]
    directions, capacity = sent_ref.shape
    pad_ref[...] = jnp.zeros(pad_ref.shape, f32)
    row_ref[...] = jnp.zeros(row_ref.shape, i32)
    row_ref[0:directions, 0:capacity] = sent_ref[...]
    head = 3 * own_blocks
    list_rows = list_ref.shape[1] - 4
    for s, ref in enumerate(given):
        slot = ref[head : head + 2 * list_rows].astype(i32)
        block = jnp.full(slot.shape, block_total, i32)
        for k in range(directions):
            here = (slot >= k * capacity) & (slot < (k + 1) * capacity)
            row = jnp.broadcast_to(row_ref[k : k + 1, :], slot.shape)
            at = jnp.where(here, slot - k * capacity, 0)
            block = jnp.where(here, jnp.take_along_axis(row, at, axis=1), block)
        rest = ref[head + 2 * list_rows :].astype(i32)
        list_ref[s, 0:list_rows] = coded(rest[0:list_rows], block[0:list_rows], block[list_rows:])
        list_ref[s, list_rows:] = rest[list_rows:]
    sent = pltpu.make_async_copy(list_ref, smem_ref, arrival)
    sent.start()
    for s, ref in enumerate(given):

        def some_targets(n, _):
            for q in range(slots):
                t = n * slots + q
                for r in range(3):
                    row = ref[pl.ds(r * own_blocks + t, 1), :]
                    pad_ref[q, r : r + 1, :] = (row - centre_km) * scale
                offsets = pad_ref[q]
                norm = -0.5 * jnp.sum(offsets * offsets, axis=0, keepdims=True)
                target_ref[s * own_blocks + t] = target_features(offsets, norm)
            return 0

        lax.fori_loop(0, own_blocks // slots, some_targets, 0)
    sent.wait()


def halo_features(sent, given, block_total, own_blocks):
    list_rows = (given[0].shape[0] - 3 * own_blocks) // 4
    lists = (len(given), list_rows + 4, BLOCK)
    return pl.pallas_call(
        functools.partial(halo_features_kernel, block_total, own_blocks),
        out_shape=(
            pltpu.VMEM((len(given) * own_blocks, FEATURES, BLOCK), bf16),
            pltpu.SMEM(lists, i32),
        ),
        in_specs=[vmem()] * (len(given) + 1),
        out_specs=(vmem(), smem()),
        scratch_shapes=[
            pltpu.VMEM(lists, i32),
            pltpu.VMEM((16, 8, BLOCK), f32),
            pltpu.VMEM((8, BLOCK), i32),
            pltpu.SemaphoreType.DMA,
        ],
        compiler_params=params(8),
        cost_estimate=lasting(1),
        name="halo_features",
    )(sent, *given)


def value_rows(first, second):
    row = lax.broadcasted_iota(i32, (8, BLOCK), 0)
    both = jnp.where((row & 1) == 1, first, second)
    high, middle, low = split(both)
    rows = jnp.where(row < 5, jnp.where(row < 3, high, middle), jnp.where(row < 7, low, 0.0))
    rows = jnp.where(row == 0, 1.0, rows).astype(bf16)
    return jnp.concatenate([rows, rows], axis=1)


def half_kernel(event_ref, mine_ref, near_ref, out_ref):
    half = out_ref.shape[1]
    at = pl.ds(pl.multiple_of((event_ref[0] & 1) * half, half), half)
    out_ref[...] = mine_ref[...] + near_ref[:, at]


def half_sum(event, mine, near):
    return pl.pallas_call(
        half_kernel,
        out_shape=jax.ShapeDtypeStruct(mine.shape, f32),
        in_specs=[smem(), vmem(), vmem()],
        out_specs=vmem(),
        compiler_params=params(4),
        cost_estimate=lasting(0.1),
        name="half_sum",
    )(event, *held(mine), near)


def add_kernel(first_ref, second_ref, mark_ref, out_ref):
    out_ref[...] = first_ref[...] + second_ref[...]


def added(first, second, mark):
    return pl.pallas_call(
        add_kernel,
        out_shape=jax.ShapeDtypeStruct(first.shape, f32),
        in_specs=[vmem()] * 3,
        out_specs=vmem(),
        compiler_params=params(4),
        cost_estimate=lasting(0.1),
        name="added",
    )(first, second, mark)


def values_kernel(event_ref, *refs):
    *given, value_ref = refs
    piece_blocks = given[0].shape[1] // BLOCK
    for piece, ref in enumerate(given):
        start = 0 if len(given) == 1 else ((event_ref[0] + piece) & 1) * piece_blocks

        def one_block(b, _):
            at = pl.ds(pl.multiple_of(b * BLOCK, BLOCK), BLOCK)
            value_ref[start + b] = value_rows(ref[0:1, at], ref[1:2, at])
            return 0

        lax.fori_loop(0, piece_blocks, one_block, 0, unroll=16)
    value_ref[value_ref.shape[0] - 1] = jnp.zeros((8, 2 * BLOCK), bf16)


def values_table(event, given, block_total):
    return pl.pallas_call(
        values_kernel,
        out_shape=pltpu.VMEM((block_total + 1, 8, 2 * BLOCK), bf16),
        in_specs=[smem()] + [vmem()] * len(given),
        out_specs=vmem(),
        compiler_params=params(8),
        cost_estimate=lasting(1),
        name="values_table",
    )(event, *given)


def totals_kernel(own_blocks, list_ref, source_ref, target_ref, value_ref, *refs):
    *out_refs, sum_ref, weight_ref, exponent_ref = refs
    sets, list_rows = list_ref.shape[0], list_ref.shape[1] - 4
    total_steps = list_ref[0, list_rows, 0]
    for s in range(1, sets):
        total_steps = total_steps + list_ref[s, list_rows, 0]

    def chunk(s, k, c):
        at = k * STEP + c
        t, first, second = decoded(list_ref[s, at >> 7, at & (BLOCK - 1)])
        return s * own_blocks + t, first, second

    def following(s, k):
        ends = k + 1 >= list_ref[s, list_rows, 0]
        after = jnp.minimum(jnp.where(ends, s + 1, s), sets - 1)
        return after, jnp.where(ends, 0, k + 1)

    def exponents(s, k, c):
        t, first, second = chunk(s, k, c)
        both = jnp.concatenate([source_ref[first], source_ref[second]], axis=0)
        exponent = jnp.dot(both, target_ref[t], preferred_element_type=f32)
        exponent_ref[c, :, 0:BLOCK] = exponent[0:BLOCK]
        exponent_ref[c, :, BLOCK:] = exponent[BLOCK:]

    def weights(c):
        weight = jnp.exp2(exponent_ref[c])
        high = weight.astype(bf16)
        weight_ref[c, 0:BLOCK] = high
        weight_ref[c, BLOCK : 2 * BLOCK] = (weight - high.astype(f32)).astype(bf16)

    def sums(s, k, c):
        t, first, second = chunk(s, k, c)
        values = jnp.concatenate([value_ref[first], value_ref[second]], axis=0)
        both = jnp.dot(values, weight_ref[c], preferred_element_type=f32)
        at = pl.ds(pl.multiple_of(t * 8, 8), 8)
        sum_ref[at, :] += both[0:8, 0:BLOCK] + both[8:16, BLOCK : 2 * BLOCK]

    sum_ref[...] = jnp.zeros(sum_ref.shape, f32)
    zero = jnp.int32(0)
    for c in range(STEP):
        exponents(zero, zero, c)

    def step(_, at):
        s, k, s_next, k_next = at
        for c in range(STEP):
            weights(c)
            sums(s, k, c)
            exponents(s_next, k_next, c)
        return s_next, k_next, *following(s_next, k_next)

    lax.fori_loop(0, total_steps, step, (zero, zero, *following(zero, zero)))

    for s in range(sets):
        rows = [
            sum_ref[pl.ds(s * own_blocks * 8 + r, own_blocks, stride=8), :] for r in range(7)
        ]
        out_refs[s][0] = rows[0]
        out_refs[s][1] = rows[1] + rows[3] + rows[5]
        out_refs[s][2] = rows[2] + rows[4] + rows[6]


def totals_of(name, lists, sources, targets, values, own_blocks):
    sets = lists.shape[0]
    return pl.pallas_call(
        functools.partial(totals_kernel, own_blocks),
        out_shape=(jax.ShapeDtypeStruct((3, own_blocks, BLOCK), f32),) * sets,
        in_specs=[smem(), vmem(), vmem(), vmem()],
        out_specs=(vmem(),) * sets,
        scratch_shapes=[
            pltpu.VMEM((sets * own_blocks * 8, BLOCK), f32),
            pltpu.VMEM((STEP, 2 * BLOCK, 2 * BLOCK), bf16),
            pltpu.VMEM((STEP, BLOCK, 2 * BLOCK), f32),
        ],
        compiler_params=params(14),
        cost_estimate=lasting(8),
        name=name,
    )(pltpu.with_memory_space_constraint(lists, pltpu.SMEM), *held(sources, targets, values))


def local(partials, coords, volume, send_blocks, halo_counts, source_slots, source_counts):
    cut_count = lax.axis_size("cuts")
    event_count = lax.axis_size("event")
    block_total = volume.shape[0] // BLOCK
    own_blocks = source_slots.shape[2]
    grid_step = cut_count // 4
    my_event = lax.axis_index("event")

    strides = [(1, [[0], [1]])]
    if grid_step == 1:
        strides = [(1, [[0, 2], [1, 3]])]
    else:
        strides.append((grid_step, [[2], [3]]))
    event = my_event.reshape(1)
    mine = partials[0]
    near_coords, near_volume, near_mine, own_lists, *parcels = prepare(
        strides, send_blocks.shape[3], event, lax.axis_index("cuts").reshape(1), halo_counts[0],
        source_slots[0, 0].T, source_counts[0], coords, volume.reshape(block_total, BLOCK),
        mine,
    )
    turns = [(stride, turn) for stride, _ in strides for turn in range(2)]
    arrived = [swapped(p, *turn) for p, turn in zip(parcels, turns)]

    sources, targets, mark = own_features(event, near_coords, near_volume, own_blocks)
    if event_count == 4:
        part = half_sum(event, near_mine, crossed(mine, "event", 1))
        part = added(part, crossed(part, "event", 2), mark)
        summed = [part, crossed(part, "event", 1)]
    else:
        summed = [lax.psum(mine, "event")]

    halo_targets, halo_lists = halo_features(
        send_blocks[0, 0], arrived, block_total, own_blocks
    )
    values = values_table(event, summed, block_total)
    halo_totals = totals_of("halo_totals", halo_lists, sources, halo_targets, values, own_blocks)
    returned = [swapped(t, *turn) for t, turn in zip(halo_totals, turns)]
    own_totals = totals_of("own_totals", own_lists, sources, targets, values, own_blocks)
    totals = own_totals[0]
    for part in returned:
        totals = totals + part
    return (totals[1:3] / totals[0]).reshape(2, own_blocks * BLOCK)


def solution(mesh):
    placed = (
        P("event", None, ("runs", "cuts")),
        P(None, ("runs", "cuts")),
        P(("runs", "cuts")),
        P(("runs", "cuts"), "event", None, None),
        P(("runs", "cuts"), "event", None),
        P(("runs", "cuts"), "event", None, None),
        P(("runs", "cuts"), "event", None),
    )
    return jax.shard_map(
        local,
        mesh=mesh,
        in_specs=placed,
        out_specs=P(None, ("runs", "cuts", "event")),
        check_vma=False,
    )
```

profile of v0, /device:TPU:0, one launch (start us, length us, event | category | flops | bytes accessed | tf_op | source)
XLA Modules:
  0.0 32.9 jit_solution(3816308099072904899)
XLA Ops:
  0.0 0.5 %collective-permute-start = (f32[2,32768]{1,0:T(2,128)}, f32[2,32768]{1,0:T(2,128)S(1)}, u32[]{:S(2)}, u32[]{:S(2)}) collective-permute-start(f32[2,32768]{1,0:T(2,128)} %bitcast.18), channel_id=1, source_target_pairs={{1,0},{0,1},{3,2},{2,3},{5,4},{4,5},{7,6},{6,7},{9,8},{8,9},{11,10... | collective-permute-start | bytes 786440 | tf_op jit(solution)/shard_map/ppermute | solution.py:59
  0.5 1.9 %prepare.1 = (f32[3,32768]{1,0:T(4,128)S(1)}, f32[256,128]{1,0:T(8,128)S(1)}, f32[2,16384]{1,0:T(2,128)S(1)}, s32[1,8,128]{2,1,0:T(8,128)S(4)}, f32[208,128]{1,0:T(8,128)S(1)}, /*index=5*/f32[208,128]{1,0:T(8,128)S(1)}) custom-call(s32[1]{0:T(128)} %bitcast.event_ref, s32[1]{0:T(128)} %bitcast.1.cut_ref, s32[1,4]{1,0:T(1,128)} %bitcast.22, ...), custom_call_target="tpu_custom_call" | custom-call | flops 2300000000 | bytes 1000000 | tf_op jit(solution)/shard_map/prepare/pallas_call | solution.py:269
  2.4 2.6 %collective-permute-start.3 = (f32[208,128]{1,0:T(8,128)S(1)}, f32[208,128]{1,0:T(8,128)S(1)}, u32[]{:S(2)}, u32[]{:S(2)}) collective-permute-start(f32[208,128]{1,0:T(8,128)S(1)} %get-tuple-element.25), channel_id=1, source_target_pairs={{0,4},{4,0},{8,12},{12,8},{1,5},{5,1},{9,13},{13,9},{2,6},{6,2},{1... | collective-permute-start | bytes 319496 | tf_op jit(solution)/shard_map/ppermute | solution.py:54
  5.0 2.5 %collective-permute-start.4 = (f32[208,128]{1,0:T(8,128)S(1)}, f32[208,128]{1,0:T(8,128)S(1)}, u32[]{:S(2)}, u32[]{:S(2)}) collective-permute-start(f32[208,128]{1,0:T(8,128)S(1)} %get-tuple-element.26), channel_id=1, source_target_pairs={{0,12},{4,8},{8,4},{12,0},{1,13},{5,9},{9,5},{13,1},{2,14},{6,10},... | collective-permute-start | bytes 319496 | tf_op jit(solution)/shard_map/ppermute | solution.py:54
  7.5 0.0 collective-permute-done.near_ref
  7.5 1.6 %collective-permute-start.1 = (f32[2,16384]{1,0:T(2,128)S(1)}, f32[2,16384]{1,0:T(2,128)S(1)}, u32[]{:S(2)}, u32[]{:S(2)}) collective-permute-start(f32[2,16384]{1,0:T(2,128)S(1)} %half_sum.1.first_ref), channel_id=1, source_target_pairs={{2,0},{3,1},{0,2},{1,3},{6,4},{7,5},{4,6},{5,7},{10,8},{11,9},{8,1... | collective-permute-start | bytes 393224 | tf_op jit(solution)/shard_map/ppermute | solution.py:59
  9.1 0.0 copy-start
  9.1 3.9 %own_features.1 = (bf16[257,128,48]{2,1,0:T(8,128)(2,1)S(1)}, bf16[64,48,128]{2,1,0:T(8,128)(2,1)S(1)}, f32[8,128]{1,0:T(8,128)S(1)}) custom-call(s32[1]{0:T(128)} %bitcast.event_ref, f32[3,32768]{1,0:T(4,128)S(1)} %get-tuple-element.19.coords_ref, f32[256,128]{1,0:T(8,128)S(1)} %get-tuple-element.20.volume_ref), custom_call_target="tpu_custom_call" | custom-call | flops 4600000000 | bytes 1000000 | tf_op jit(solution)/shard_map/own_features/pallas_call | solution.py:121
  13.0 0.0 collective-permute-done.1.second_ref
  13.1 0.1 collective-permute-start.2
  13.2 0.0 collective-permute-done.3.refs_0_
  13.2 0.1 collective-permute-done.4.refs_1_
  13.3 0.0 copy-done
  13.3 0.8 %halo_features.1 = (bf16[128,48,128]{2,1,0:T(8,128)(2,1)S(1)}, s32[2,8,128]{2,1,0:T(8,128)S(4)}) custom-call(s32[4,64]{1,0:T(4,128)S(1)} %bitcast.17, f32[208,128]{1,0:T(8,128)S(1)} %collective-permute-done.3.refs_0_, f32[208,128]{1,0:T(8,128)S(1)} %collective-permute-done.4.refs_1_), custom_call_target="tpu_custom_call" | custom-call | flops 1150000000 | bytes 1000000 | tf_op jit(solution)/shard_map/halo_features/pallas_call | solution.py:336
  14.1 0.4 %collective-permute-done.2.refs_1_ = f32[2,16384]{1,0:T(2,128)S(1)} collective-permute-done((f32[2,16384]{1,0:T(2,128)S(1)}, f32[2,16384]{1,0:T(2,128)S(1)}, u32[]{:S(2)}, u32[]{:S(2)}) %collective-permute-start.2) | collective-permute-done | bytes 131104 | tf_op jit(solution)/shard_map/ppermute | solution.py:59
  14.5 0.6 %values_table.1.value_ref = bf16[257,8,256]{2,1,0:T(8,128)(2,1)S(1)} custom-call(s32[1]{0:T(128)} %bitcast.event_ref, f32[2,16384]{1,0:T(2,128)S(1)} %added.1.refs_0_, f32[2,16384]{1,0:T(2,128)S(1)} %collective-permute-done.2.refs_1_), custom_call_target="tpu_custom_call" | custom-call | flops 1150000000 | bytes 1000000 | tf_op jit(solution)/shard_map/values_table/pallas_call | solution.py:415
  15.1 5.8 %halo_totals.1 = (f32[3,64,128]{2,1,0:T(8,128)S(1)}, f32[3,64,128]{2,1,0:T(8,128)S(1)}) custom-call(s32[2,8,128]{2,1,0:T(8,128)S(4)} %get-tuple-element.27.list_ref, bf16[257,128,48]{2,1,0:T(8,128)(2,1)S(1)} %get-tuple-element.21.source_ref, bf16[128,48,128]{2,1,0:T(8,128)(2,1)S(1)} %get-tuple-element.28.target_ref, ...), custom_call_target="tpu_custom_call" | custom-call | flops 9200000000 | bytes 1000000 | tf_op jit(solution)/shard_map/halo_totals/pallas_call | solution.py:489
  20.8 1.3 %collective-permute-start.5 = (f32[3,64,128]{2,1,0:T(8,128)S(1)}, f32[3,64,128]{2,1,0:T(8,128)S(1)}, u32[]{:S(2)}, u32[]{:S(2)}) collective-permute-start(f32[3,64,128]{2,1,0:T(8,128)S(1)} %get-tuple-element.29), channel_id=1, source_target_pairs={{0,4},{4,0},{8,12},{12,8},{1,5},{5,1},{9,13},{13,9},{2,6},{6,2},{1... | collective-permute-start | bytes 294920 | tf_op jit(solution)/shard_map/ppermute | solution.py:54
  22.1 1.6 %collective-permute-start.6 = (f32[3,64,128]{2,1,0:T(8,128)S(1)}, f32[3,64,128]{2,1,0:T(8,128)S(1)}, u32[]{:S(2)}, u32[]{:S(2)}) collective-permute-start(f32[3,64,128]{2,1,0:T(8,128)S(1)} %get-tuple-element.30), channel_id=1, source_target_pairs={{0,12},{4,8},{8,4},{12,0},{1,13},{5,9},{9,5},{13,1},{2,14},{6,10},... | collective-permute-start | bytes 294920 | tf_op jit(solution)/shard_map/ppermute | solution.py:54
  23.7 8.4 %own_totals.1 = f32[3,64,128]{2,1,0:T(8,128)S(1)} custom-call(s32[1,8,128]{2,1,0:T(8,128)S(4)} %get-tuple-element.18.list_ref, bf16[257,128,48]{2,1,0:T(8,128)(2,1)S(1)} %get-tuple-element.21.source_ref, bf16[64,48,128]{2,1,0:T(8,128)(2,1)S(1)} %get-tuple-element.22.target_ref, bf16[257,8,256]{2,1,0:T(8,128)(2,1)S(1)} %values_table.1.value_ref), custom_call_target="tpu_custom_call" | custom-call | flops 9200000000 | bytes 1000000 | tf_op jit(solution)/shard_map/own_totals/pallas_call | solution.py:489
  32.1 0.0 collective-permute-done.5
  32.1 0.0 collective-permute-done.6
  32.2 0.7 %copy.10 = f32[1,2,64,128]{3,1,2,0:T(2,128)} copy(f32[1,2,64,128]{3,2,1,0:T(8,128)S(1)} %fusion) | data formatting | bytes 131072
  (5 shorter events, 0.1 us)
Async XLA Ops:
  0.0 7.5 %collective-permute-start = (f32[2,32768]{1,0:T(2,128)}, f32[2,32768]{1,0:T(2,128)S(1)}, u32[]{:S(2)}, u32[]{:S(2)}) collective-permute-start(f32[2,32768]{1,0:T(2,128)} %bitcast.18), channel_id=1, source_target_pairs={{1,0},{0,1},{3,2},{2,3},{5,4},{4,5},{7,6},{6,7},{9,8},{8,9},{11,10... | collective-permute-start | bytes 786440 | tf_op jit(solution)/shard_map/ppermute | solution.py:59
  2.4 10.8 %collective-permute-start.3 = (f32[208,128]{1,0:T(8,128)S(1)}, f32[208,128]{1,0:T(8,128)S(1)}, u32[]{:S(2)}, u32[]{:S(2)}) collective-permute-start(f32[208,128]{1,0:T(8,128)S(1)} %get-tuple-element.25), channel_id=1, source_target_pairs={{0,4},{4,0},{8,12},{12,8},{1,5},{5,1},{9,13},{13,9},{2,6},{6,2},{1... | collective-permute-start | bytes 319496 | tf_op jit(solution)/shard_map/ppermute | solution.py:54
  5.0 8.2 %collective-permute-start.4 = (f32[208,128]{1,0:T(8,128)S(1)}, f32[208,128]{1,0:T(8,128)S(1)}, u32[]{:S(2)}, u32[]{:S(2)}) collective-permute-start(f32[208,128]{1,0:T(8,128)S(1)} %get-tuple-element.26), channel_id=1, source_target_pairs={{0,12},{4,8},{8,4},{12,0},{1,13},{5,9},{9,5},{13,1},{2,14},{6,10},... | collective-permute-start | bytes 319496 | tf_op jit(solution)/shard_map/ppermute | solution.py:54
  7.5 5.5 %collective-permute-start.1 = (f32[2,16384]{1,0:T(2,128)S(1)}, f32[2,16384]{1,0:T(2,128)S(1)}, u32[]{:S(2)}, u32[]{:S(2)}) collective-permute-start(f32[2,16384]{1,0:T(2,128)S(1)} %half_sum.1.first_ref), channel_id=1, source_target_pairs={{2,0},{3,1},{0,2},{1,3},{6,4},{7,5},{4,6},{5,7},{10,8},{11,9},{8,1... | collective-permute-start | bytes 393224 | tf_op jit(solution)/shard_map/ppermute | solution.py:59
  9.1 4.2 %copy-start = (s32[1,1,4,64]{3,2,1,0:T(4,128)S(1)}, s32[1,1,4,64]{3,2,1,0:T(4,128)}, u32[]{:S(2)}) copy-start(s32[1,1,4,64]{3,2,1,0:T(4,128)} %param.10) | copy-start | bytes 3076
  13.1 1.4 %collective-permute-start.2 = (f32[2,16384]{1,0:T(2,128)S(1)}, f32[2,16384]{1,0:T(2,128)S(1)}, u32[]{:S(2)}, u32[]{:S(2)}) collective-permute-start(f32[2,16384]{1,0:T(2,128)S(1)} %added.1.refs_0_), channel_id=1, source_target_pairs={{1,0},{0,1},{3,2},{2,3},{5,4},{4,5},{7,6},{6,7},{9,8},{8,9},{11,10... | collective-permute-start | bytes 393224 | tf_op jit(solution)/shard_map/ppermute | solution.py:59
  20.8 11.2 %collective-permute-start.5 = (f32[3,64,128]{2,1,0:T(8,128)S(1)}, f32[3,64,128]{2,1,0:T(8,128)S(1)}, u32[]{:S(2)}, u32[]{:S(2)}) collective-permute-start(f32[3,64,128]{2,1,0:T(8,128)S(1)} %get-tuple-element.29), channel_id=1, source_target_pairs={{0,4},{4,0},{8,12},{12,8},{1,5},{5,1},{9,13},{13,9},{2,6},{6,2},{1... | collective-permute-start | bytes 294920 | tf_op jit(solution)/shard_map/ppermute | solution.py:54
  22.1 10.0 %collective-permute-start.6 = (f32[3,64,128]{2,1,0:T(8,128)S(1)}, f32[3,64,128]{2,1,0:T(8,128)S(1)}, u32[]{:S(2)}, u32[]{:S(2)}) collective-permute-start(f32[3,64,128]{2,1,0:T(8,128)S(1)} %get-tuple-element.30), channel_id=1, source_target_pairs={{0,12},{4,8},{8,4},{12,0},{1,13},{5,9},{9,5},{13,1},{2,14},{6,10},... | collective-permute-start | bytes 294920 | tf_op jit(solution)/shard_map/ppermute | solution.py:54
where the time goes:
time: 33 us; the launch traced here: 32.9 us
  Pallas kernels  21.4 us (65%)
  starting transfers between devices  10.1 us (31%)
  local copies, waits for them, and re-layouts  0.69 us (2%)
  waiting for transfers between devices  0.53 us (2%)
    pallas_call x2, Pallas kernels, totals_of(): pl.pallas_call(functools.partial(totals_kernel, own_blocks), out_shape=(j...  14.1 us
    ppermute x4, starting transfers between devices, swapped(): return lax.ppermute(block, 'cuts', route)  7.99 us
    pallas_call x1, Pallas kernels, own_features(): pl.pallas_call(own_features_kernel, out_shape=(pltpu.VMEM((block_total +...  3.94 us
    ppermute x3, starting transfers between devices, crossed(): return lax.ppermute(block, axis, route)  2.08 us
    pallas_call x1, Pallas kernels, prepare(): pl.pallas_call(functools.partial(prepare_kernel, strides, capacity), out_...  1.94 us
    pallas_call x1, Pallas kernels, halo_features(): pl.pallas_call(functools.partial(halo_features_kernel, block_total, own_b...  0.79 us
    unnamed x3, local copies, waits for them, and re-layouts  0.69 us
  transfers between devices with their start and end apart: 7, of which 2 were waited for; matrix products, arithmetic and copies ran while one was open for 0% of the time, Pallas kernels for 46%

commit v1 on v0

--- a/solution.py
+++ b/solution.py
@@ -10,8 +10,9 @@
 
 BLOCK = 128
 FEATURES = 48
-STEP_BITS = 4
+STEP_BITS = 5
 STEP = 1 << STEP_BITS
+QUOTA = 6
 FIELD = 10
 sigma_km = 50.0
 centre_km = 400.0
@@ -127,7 +128,10 @@
         ),
         in_specs=[smem(), vmem(), vmem()],
         out_specs=(vmem(),) * 3,
-        scratch_shapes=[pltpu.VMEM((16, 8, BLOCK), f32), pltpu.VMEM((block_total, BLOCK), f32)],
+        scratch_shapes=[
+            pltpu.VMEM((16, 8, BLOCK), f32),
+            pltpu.VMEM((block_total, BLOCK), f32),
+        ],
         compiler_params=params(8),
         cost_estimate=lasting(4),
         name="own_features",
@@ -136,6 +140,13 @@
 
 def coded(target, first, second):
     return (target << (2 * FIELD)) + (second << FIELD) + first
+
+
+def finished_list(ref, codes, spare, count):
+    list_rows = codes.shape[0]
+    ref[0:list_rows] = codes
+    ref[list_rows : list_rows + 1] = jnp.full((1, BLOCK), coded(0, spare, spare), i32)
+    ref[list_rows + 1 :] = count[0:3]
 
 
 def decoded(code):
@@ -148,7 +159,7 @@
     volume_given, mine_given, coords_ref, volume_ref, mine_ref, own_ref, *refs,
 ):
     parcels, rest = refs[: 2 * len(strides)], refs[2 * len(strides) :]
-    halo_ref, slot_ref, count_ref, row_ref, list_ref, arrival = rest
+    halo_ref, slot_ref, count_ref, row_ref, arrival = rest
     width, own_blocks = slot_ref.shape
     block_total = volume_ref.shape[0]
     sets = len(parcels) + 1
@@ -183,7 +194,7 @@
                 live = live + (near & (halo < (k + 1) * capacity)).astype(i32)
             both.append(live)
         odd = (cut_ref[0] // stride) % 2
-        for first, second in (both[::-1], both):
+        for first, second in (both, both[::-1]):
             live = first * (1 - odd) + second * odd
             lives.append(used & (live > 0))
     rows = sets * width
@@ -236,17 +247,14 @@
         part = slice(s * list_rows, (s + 1) * list_rows)
         spare = block_total if s == 0 else 4 * capacity
         pair = [jnp.where(b[part] < 0, spare, b[part]) for b in blocks]
-        steps = jnp.maximum((total[s * width : s * width + 4] + STEP - 1) >> STEP_BITS, 1)
+        count = total[s * width : s * width + list_rows]
         if s == 0:
-            list_ref[0, 0:list_rows] = coded(target[part], *pair)
-            list_ref[0, list_rows:] = steps
+            finished_list(own_ref, coded(target[part], *pair), spare, count)
         else:
-            given = [*pair, target[part], steps]
+            given = [*pair, target[part], count]
             for n, values in enumerate(given):
                 at = 3 * own_blocks + n * list_rows
                 parcels[s - 1][at : at + list_rows] = values.astype(f32)
-    sent = pltpu.make_async_copy(list_ref, own_ref, arrival.at[6])
-    sent.start()
     for copy in brought[3:]:
         copy.wait()
 
@@ -259,7 +267,6 @@
         return 0
 
     lax.fori_loop(0, own_blocks, some_coords, 0, unroll=8)
-    sent.wait()
 
 
 def prepare(strides, capacity, event, cut, halo_counts, slots, counts, coords, volume, mine):
@@ -272,18 +279,17 @@
             pltpu.VMEM(coords.shape, f32),
             pltpu.VMEM(volume.shape, f32),
             pltpu.VMEM((2, mine.shape[1] // 2), f32),
-            pltpu.SMEM((1, list_rows + 4, BLOCK), i32),
+            pltpu.VMEM((list_rows + 4, BLOCK), i32),
         )
         + (parcel,) * (2 * len(strides)),
         in_specs=[smem()] * 2 + [pl.BlockSpec(memory_space=pltpu.HBM)] * 6,
-        out_specs=(vmem(), vmem(), vmem(), smem()) + (vmem(),) * (2 * len(strides)),
+        out_specs=(vmem(),) * 4 + (vmem(),) * (2 * len(strides)),
         scratch_shapes=[
             pltpu.SMEM(halo_counts.shape, i32),
             pltpu.VMEM(slots.shape, i32),
             pltpu.VMEM(counts.shape, i32),
             pltpu.VMEM((width + 8, BLOCK), i32),
-            pltpu.VMEM((1, list_rows + 4, BLOCK), i32),
-            pltpu.SemaphoreType.DMA((7,)),
+            pltpu.SemaphoreType.DMA((6,)),
         ],
         compiler_params=params(8),
         cost_estimate=lasting(2),
@@ -291,7 +297,7 @@
     )(event, cut, *far(halo_counts, slots, counts, coords, volume, mine))
 
 
-def halo_features_kernel(block_total, own_blocks, sent_ref, *refs):
+def halo_features_kernel(block_total, own_blocks, own_ref, near_ref, sent_ref, *refs):
     *given, target_ref, smem_ref, list_ref, pad_ref, row_ref, arrival = refs
     slots = pad_ref.shape[0]
     directions, capacity = sent_ref.shape
@@ -309,10 +315,12 @@
             at = jnp.where(here, slot - k * capacity, 0)
             block = jnp.where(here, jnp.take_along_axis(row, at, axis=1), block)
         rest = ref[head + 2 * list_rows :].astype(i32)
-        list_ref[s, 0:list_rows] = coded(rest[0:list_rows], block[0:list_rows], block[list_rows:])
-        list_ref[s, list_rows:] = rest[list_rows:]
+        codes = coded(rest[0:list_rows], block[0:list_rows], block[list_rows:])
+        finished_list(list_ref.at[s], codes, block_total, rest[list_rows:])
+    list_ref[len(given)] = own_ref[...]
     sent = pltpu.make_async_copy(list_ref, smem_ref, arrival)
     sent.start()
+    target_ref[len(given) * own_blocks :] = near_ref[...]
     for s, ref in enumerate(given):
 
         def some_targets(n, _):
@@ -330,16 +338,17 @@
     sent.wait()
 
 
-def halo_features(sent, given, block_total, own_blocks):
+def halo_features(own_list, targets, sent, given, block_total):
+    own_blocks = targets.shape[0]
     list_rows = (given[0].shape[0] - 3 * own_blocks) // 4
-    lists = (len(given), list_rows + 4, BLOCK)
+    lists = (len(given) + 1, list_rows + 4, BLOCK)
     return pl.pallas_call(
         functools.partial(halo_features_kernel, block_total, own_blocks),
         out_shape=(
-            pltpu.VMEM((len(given) * own_blocks, FEATURES, BLOCK), bf16),
+            pltpu.VMEM(((len(given) + 1) * own_blocks, FEATURES, BLOCK), bf16),
             pltpu.SMEM(lists, i32),
         ),
-        in_specs=[vmem()] * (len(given) + 1),
+        in_specs=[vmem()] * (len(given) + 3),
         out_specs=(vmem(), smem()),
         scratch_shapes=[
             pltpu.VMEM(lists, i32),
@@ -350,7 +359,7 @@
         compiler_params=params(8),
         cost_estimate=lasting(1),
         name="halo_features",
-    )(sent, *given)
+    )(*held(own_list, targets), sent, *given)
 
 
 def value_rows(first, second):
@@ -362,22 +371,25 @@
     return jnp.concatenate([rows, rows], axis=1)
 
 
-def half_kernel(event_ref, mine_ref, near_ref, out_ref):
+def half_kernel(event_ref, mine_ref, near_ref, *refs):
+    parcels, (out_ref, *sent) = refs[: len(refs) // 2], refs[len(refs) // 2 :]
     half = out_ref.shape[1]
     at = pl.ds(pl.multiple_of((event_ref[0] & 1) * half, half), half)
     out_ref[...] = mine_ref[...] + near_ref[:, at]
-
-
-def half_sum(event, mine, near):
+    for given, to in zip(parcels, sent):
+        to[...] = given[...]
+
+
+def half_sum(event, mine, near, parcels):
     return pl.pallas_call(
         half_kernel,
-        out_shape=jax.ShapeDtypeStruct(mine.shape, f32),
-        in_specs=[smem(), vmem(), vmem()],
-        out_specs=vmem(),
+        out_shape=[jax.ShapeDtypeStruct(a.shape, f32) for a in (mine, *parcels)],
+        in_specs=[smem()] + [vmem()] * (len(parcels) + 2),
+        out_specs=[vmem()] * (len(parcels) + 1),
         compiler_params=params(4),
         cost_estimate=lasting(0.1),
         name="half_sum",
-    )(event, *held(mine), near)
+    )(event, *held(mine), near, *parcels)
 
 
 def add_kernel(first_ref, second_ref, mark_ref, out_ref):
@@ -396,110 +408,181 @@
     )(first, second, mark)
 
 
-def values_kernel(event_ref, *refs):
-    *given, value_ref = refs
-    piece_blocks = given[0].shape[1] // BLOCK
-    for piece, ref in enumerate(given):
-        start = 0 if len(given) == 1 else ((event_ref[0] + piece) & 1) * piece_blocks
-
-        def one_block(b, _):
+def schedule(list_ref):
+    sets, list_rows = list_ref.shape[0], list_ref.shape[1] - 4
+    ends = []
+    for s in range(sets):
+        ends.append(list_ref[s, list_rows + 1, 0] + (ends[-1] if ends else 0))
+    halo_steps, all_steps = [(e + STEP - 1) >> STEP_BITS for e in ends[-2:]]
+    return ends, jnp.maximum(halo_steps, jnp.minimum(QUOTA, all_steps)), all_steps
+
+
+class Totals:
+    def __init__(self, ends, own_blocks, first_set, refs):
+        self.ends, self.own_blocks, self.first_set = ends, own_blocks, first_set
+        self.lists, self.sources, self.targets, self.values = refs[:4]
+        self.exponent_ref, self.weight_ref, self.sum_ref = refs[4:]
+
+    def chunk(self, i):
+        s, base = 0, 0
+        for end in self.ends[:-1]:
+            past = i >= end
+            s = s + past.astype(i32)
+            base = jnp.where(past, end, base)
+        at = i - base
+        t, first, second = decoded(self.lists[s, at >> 7, at & (BLOCK - 1)])
+        return s * self.own_blocks + t, first, second
+
+    def exponents(self, k, c):
+        t, first, second = self.chunk(k * STEP + c)
+        both = jnp.concatenate([self.sources[first], self.sources[second]], axis=0)
+        exponent = jnp.dot(both, self.targets[t], preferred_element_type=f32)
+        self.exponent_ref[c, :, 0:BLOCK] = exponent[0:BLOCK]
+        self.exponent_ref[c, :, BLOCK:] = exponent[BLOCK:]
+
+    def weights(self, c):
+        weight = jnp.exp2(self.exponent_ref[c])
+        high = weight.astype(bf16)
+        self.weight_ref[c, 0:BLOCK] = high
+        self.weight_ref[c, BLOCK : 2 * BLOCK] = (weight - high.astype(f32)).astype(bf16)
+
+    def sums(self, k, c):
+        t, first, second = self.chunk(k * STEP + c)
+        values = jnp.concatenate([self.values[first], self.values[second]], axis=0)
+        both = jnp.dot(values, self.weight_ref[c], preferred_element_type=f32)
+        at = pl.ds(pl.multiple_of((t - self.first_set * self.own_blocks) * 8, 8), 8)
+        self.sum_ref[at, :] += both[0:8, 0:BLOCK] + both[8:16, BLOCK : 2 * BLOCK]
+
+    def steps(self, begin, end):
+        def step(k, _):
+            for c in range(STEP):
+                self.weights(c)
+                self.sums(k, c)
+                self.exponents(k + 1, c)
+            return 0
+
+        lax.fori_loop(begin, end, step, 0)
+
+    def finish(self, s, out_ref):
+        rows = [
+            self.sum_ref[pl.ds(s * self.own_blocks * 8 + r, self.own_blocks, stride=8), :]
+            for r in range(7)
+        ]
+        out_ref[0] = rows[0]
+        out_ref[1] = rows[1] + rows[3] + rows[5]
+        out_ref[2] = rows[2] + rows[4] + rows[6]
+
+
+def first_totals_kernel(own_blocks, list_ref, source_ref, target_ref, *refs):
+    *refs, sum_ref, weight_ref = refs
+    sets = list_ref.shape[0]
+    own_sum_ref, value_ref, exponent_ref = refs[-3:]
+    out_refs = refs[-3 - (sets - 1) : -3]
+    summed = refs[: -3 - (sets - 1)]
+    ends, first_steps, _ = schedule(list_ref)
+    given = [list_ref, source_ref, target_ref, value_ref, exponent_ref, weight_ref, sum_ref]
+    totals = Totals(ends, own_blocks, 0, given)
+    sum_ref[...] = jnp.zeros(sum_ref.shape, f32)
+    block_total = value_ref.shape[0] - 1
+    rounds = 1
+
+    def begin(n, _):
+        for c in range(STEP // rounds):
+            totals.exponents(0, n * (STEP // rounds) + c)
+        for c in range(block_total // rounds):
+            b = n * (block_total // rounds) + c
             at = pl.ds(pl.multiple_of(b * BLOCK, BLOCK), BLOCK)
-            value_ref[start + b] = value_rows(ref[0:1, at], ref[1:2, at])
-            return 0
-
-        lax.fori_loop(0, piece_blocks, one_block, 0, unroll=16)
-    value_ref[value_ref.shape[0] - 1] = jnp.zeros((8, 2 * BLOCK), bf16)
-
-
-def values_table(event, given, block_total):
+            both = sum(ref[:, at] for ref in summed)
+            value_ref[b] = value_rows(both[0:1], both[1:2])
+        return 0
+
+    if len(summed) == 1:
+        lax.fori_loop(0, rounds, begin, 0)
+    else:
+        begin_from_halves(totals, summed, value_ref, rounds)
+    value_ref[block_total] = jnp.zeros((8, 2 * BLOCK), bf16)
+    totals.steps(0, first_steps)
+    for s in range(sets - 1):
+        totals.finish(s, out_refs[s])
+    own_sum_ref[...] = sum_ref[(sets - 1) * own_blocks * 8 :, :]
+
+
+def begin_from_halves(totals, summed, value_ref, rounds):
+    event_ref, *halves = summed
+    half_blocks = (value_ref.shape[0] - 1) // 2
+    core = event_ref[0] & 1
+
+    def begin(n, _):
+        for c in range(STEP // rounds):
+            totals.exponents(0, n * (STEP // rounds) + c)
+        for piece, ref in enumerate(halves):
+            for c in range(half_blocks // rounds):
+                b = n * (half_blocks // rounds) + c
+                at = pl.ds(pl.multiple_of(b * BLOCK, BLOCK), BLOCK)
+                where = (core ^ piece) * half_blocks + b
+                totals.values[where] = value_rows(ref[0:1, at], ref[1:2, at])
+        return 0
+
+    lax.fori_loop(0, rounds, begin, 0)
+
+
+def first_totals(lists, sources, targets, summed, block_total):
+    sets = lists.shape[0]
+    own_blocks = targets.shape[0] // sets
+    specs = [smem()] * (len(summed) - 2) + [vmem()] * min(len(summed), 2)
     return pl.pallas_call(
-        values_kernel,
-        out_shape=pltpu.VMEM((block_total + 1, 8, 2 * BLOCK), bf16),
-        in_specs=[smem()] + [vmem()] * len(given),
-        out_specs=vmem(),
-        compiler_params=params(8),
-        cost_estimate=lasting(1),
-        name="values_table",
-    )(event, *given)
-
-
-def totals_kernel(own_blocks, list_ref, source_ref, target_ref, value_ref, *refs):
-    *out_refs, sum_ref, weight_ref, exponent_ref = refs
-    sets, list_rows = list_ref.shape[0], list_ref.shape[1] - 4
-    total_steps = list_ref[0, list_rows, 0]
-    for s in range(1, sets):
-        total_steps = total_steps + list_ref[s, list_rows, 0]
-
-    def chunk(s, k, c):
-        at = k * STEP + c
-        t, first, second = decoded(list_ref[s, at >> 7, at & (BLOCK - 1)])
-        return s * own_blocks + t, first, second
-
-    def following(s, k):
-        ends = k + 1 >= list_ref[s, list_rows, 0]
-        after = jnp.minimum(jnp.where(ends, s + 1, s), sets - 1)
-        return after, jnp.where(ends, 0, k + 1)
-
-    def exponents(s, k, c):
-        t, first, second = chunk(s, k, c)
-        both = jnp.concatenate([source_ref[first], source_ref[second]], axis=0)
-        exponent = jnp.dot(both, target_ref[t], preferred_element_type=f32)
-        exponent_ref[c, :, 0:BLOCK] = exponent[0:BLOCK]
-        exponent_ref[c, :, BLOCK:] = exponent[BLOCK:]
-
-    def weights(c):
-        weight = jnp.exp2(exponent_ref[c])
-        high = weight.astype(bf16)
-        weight_ref[c, 0:BLOCK] = high
-        weight_ref[c, BLOCK : 2 * BLOCK] = (weight - high.astype(f32)).astype(bf16)
-
-    def sums(s, k, c):
-        t, first, second = chunk(s, k, c)
-        values = jnp.concatenate([value_ref[first], value_ref[second]], axis=0)
-        both = jnp.dot(values, weight_ref[c], preferred_element_type=f32)
-        at = pl.ds(pl.multiple_of(t * 8, 8), 8)
-        sum_ref[at, :] += both[0:8, 0:BLOCK] + both[8:16, BLOCK : 2 * BLOCK]
-
-    sum_ref[...] = jnp.zeros(sum_ref.shape, f32)
-    zero = jnp.int32(0)
-    for c in range(STEP):
-        exponents(zero, zero, c)
-
-    def step(_, at):
-        s, k, s_next, k_next = at
-        for c in range(STEP):
-            weights(c)
-            sums(s, k, c)
-            exponents(s_next, k_next, c)
-        return s_next, k_next, *following(s_next, k_next)
-
-    lax.fori_loop(0, total_steps, step, (zero, zero, *following(zero, zero)))
-
-    for s in range(sets):
-        rows = [
-            sum_ref[pl.ds(s * own_blocks * 8 + r, own_blocks, stride=8), :] for r in range(7)
-        ]
-        out_refs[s][0] = rows[0]
-        out_refs[s][1] = rows[1] + rows[3] + rows[5]
-        out_refs[s][2] = rows[2] + rows[4] + rows[6]
-
-
-def totals_of(name, lists, sources, targets, values, own_blocks):
-    sets = lists.shape[0]
-    return pl.pallas_call(
-        functools.partial(totals_kernel, own_blocks),
-        out_shape=(jax.ShapeDtypeStruct((3, own_blocks, BLOCK), f32),) * sets,
-        in_specs=[smem(), vmem(), vmem(), vmem()],
-        out_specs=(vmem(),) * sets,
+        functools.partial(first_totals_kernel, own_blocks),
+        out_shape=[jax.ShapeDtypeStruct((3, own_blocks, BLOCK), f32)] * (sets - 1)
+        + [
+            pltpu.VMEM((own_blocks * 8, BLOCK), f32),
+            pltpu.VMEM((block_total + 1, 8, 2 * BLOCK), bf16),
+            pltpu.VMEM((STEP, BLOCK, 2 * BLOCK), f32),
+        ],
+        in_specs=[smem(), vmem(), vmem()] + specs,
+        out_specs=[vmem()] * (sets + 2),
         scratch_shapes=[
             pltpu.VMEM((sets * own_blocks * 8, BLOCK), f32),
             pltpu.VMEM((STEP, 2 * BLOCK, 2 * BLOCK), bf16),
-            pltpu.VMEM((STEP, BLOCK, 2 * BLOCK), f32),
         ],
         compiler_params=params(14),
         cost_estimate=lasting(8),
-        name=name,
-    )(pltpu.with_memory_space_constraint(lists, pltpu.SMEM), *held(sources, targets, values))
+        name="first_totals",
+    )(pltpu.with_memory_space_constraint(lists, pltpu.SMEM), *held(sources, targets), *summed)
+
+
+def last_totals_kernel(
+    own_blocks, list_ref, source_ref, target_ref, value_ref, own_sum_ref, _, out_ref,
+    exponent_ref, sum_ref, weight_ref,
+):
+    ends, first_steps, all_steps = schedule(list_ref)
+    given = [list_ref, source_ref, target_ref, value_ref, exponent_ref, weight_ref, sum_ref]
+    totals = Totals(ends, own_blocks, list_ref.shape[0] - 1, given)
+    sum_ref[...] = own_sum_ref[...]
+    totals.steps(first_steps, all_steps)
+    totals.finish(0, out_ref)
+
+
+def last_totals(lists, sources, targets, values, own_sum, exponent):
+    own_blocks = targets.shape[0] // lists.shape[0]
+    lists = pltpu.with_memory_space_constraint(lists, pltpu.SMEM)
+    total, _ = pl.pallas_call(
+        functools.partial(last_totals_kernel, own_blocks),
+        out_shape=[
+            jax.ShapeDtypeStruct((3, own_blocks, BLOCK), f32),
+            pltpu.VMEM(exponent.shape, f32),
+        ],
+        in_specs=[smem()] + [vmem()] * 5,
+        out_specs=[vmem()] * 2,
+        scratch_shapes=[
+            pltpu.VMEM((own_blocks * 8, BLOCK), f32),
+            pltpu.VMEM((STEP, 2 * BLOCK, 2 * BLOCK), bf16),
+        ],
+        input_output_aliases={5: 1},
+        compiler_params=params(14),
+        cost_estimate=lasting(8),
+        name="last_totals",
+    )(lists, *held(sources, targets, values, own_sum, exponent))
+    return total
 
 
 def local(partials, coords, volume, send_blocks, halo_counts, source_slots, source_counts):
@@ -517,30 +600,31 @@
         strides.append((grid_step, [[2], [3]]))
     event = my_event.reshape(1)
     mine = partials[0]
-    near_coords, near_volume, near_mine, own_lists, *parcels = prepare(
+    near_coords, near_volume, near_mine, own_list, *parcels = prepare(
         strides, send_blocks.shape[3], event, lax.axis_index("cuts").reshape(1), halo_counts[0],
         source_slots[0, 0].T, source_counts[0], coords, volume.reshape(block_total, BLOCK),
         mine,
     )
-    turns = [(stride, turn) for stride, _ in strides for turn in range(2)]
+    turns = [(stride, turn) for stride, _ in strides for turn in (1, 0)]
+    if event_count == 4:
+        part, *parcels = half_sum(event, near_mine, crossed(mine, "event", 1), parcels)
+        far_part = crossed(part, "event", 2)
     arrived = [swapped(p, *turn) for p, turn in zip(parcels, turns)]
-
     sources, targets, mark = own_features(event, near_coords, near_volume, own_blocks)
     if event_count == 4:
-        part = half_sum(event, near_mine, crossed(mine, "event", 1))
-        part = added(part, crossed(part, "event", 2), mark)
-        summed = [part, crossed(part, "event", 1)]
+        part = added(part, far_part, mark)
+        summed = [event, part, crossed(part, "event", 1)]
     else:
         summed = [lax.psum(mine, "event")]
 
-    halo_targets, halo_lists = halo_features(
-        send_blocks[0, 0], arrived, block_total, own_blocks
+    targets, lists = halo_features(
+        own_list, targets, send_blocks[0, 0], arrived, block_total
     )
-    values = values_table(event, summed, block_total)
-    halo_totals = totals_of("halo_totals", halo_lists, sources, halo_targets, values, own_blocks)
+    *halo_totals, own_sum, values, exponent = first_totals(
+        lists, sources, targets, summed, block_total
+    )
     returned = [swapped(t, *turn) for t, turn in zip(halo_totals, turns)]
-    own_totals = totals_of("own_totals", own_lists, sources, targets, values, own_blocks)
-    totals = own_totals[0]
+    totals = last_totals(lists, sources, targets, values, own_sum, exponent)
     for part in returned:
         totals = totals + part
     return (totals[1:3] / totals[0]).reshape(2, own_blocks * BLOCK)

time: 33 us -> 29.3 us (0.89)
  Pallas kernels: 21.4 us -> 17.3 us
  waiting for transfers between devices: 0.53 us -> 1.64 us
  starting transfers between devices: 10.1 us -> 9.07 us
    pallas_call x4 -> x3, Pallas kernels: 14.7 us -> 11 us  [the longest x1 6.45 us: first_totals(): pl.pallas_call(functools.partial(first_totals_kernel, own_blocks), out_sh...]
    ppermute x4, waiting for transfers between devices: 0.1 us -> 1.39 us  [swapped(): return lax.ppermute(block, 'cuts', route)]
    ppermute x4, starting transfers between devices: 7.99 us -> 7.06 us  [swapped(): return lax.ppermute(block, 'cuts', route)]
    pallas_call x1, Pallas kernels: 1.94 us -> 1.51 us  [prepare(): pl.pallas_call(functools.partial(prepare_kernel, strides, capacity), out_...]
  transfers between devices with their start and end apart: 7 -> 7, of which waited for: 2 -> 4; matrix products, arithmetic and copies ran while one was open for 0% -> 0% of each run, Pallas kernels for 46% -> 38%
where the time goes in v1:
time: 29.3 us; the launch traced here: 28.9 us
  Pallas kernels  17.3 us (59%)
  starting transfers between devices  9.07 us (31%)
  waiting for transfers between devices  1.64 us (6%)
  local copies, waits for them, and re-layouts  0.69 us (2%)
    ppermute x4, starting transfers between devices, swapped(): return lax.ppermute(block, 'cuts', route)  7.06 us
    pallas_call x1, Pallas kernels, first_totals(): pl.pallas_call(functools.partial(first_totals_kernel, own_blocks), out_sh...  6.45 us
    pallas_call x1, Pallas kernels, last_totals(): pl.pallas_call(functools.partial(last_totals_kernel, own_blocks), out_sha...  4.54 us
    pallas_call x1, Pallas kernels, own_features(): pl.pallas_call(own_features_kernel, out_shape=(pltpu.VMEM((block_total +...  3.95 us
    ppermute x3, starting transfers between devices, crossed(): return lax.ppermute(block, axis, route)  2.01 us
    pallas_call x1, Pallas kernels, prepare(): pl.pallas_call(functools.partial(prepare_kernel, strides, capacity), out_...  1.51 us
    ppermute x4, waiting for transfers between devices, swapped(): return lax.ppermute(block, 'cuts', route)  1.39 us
    pallas_call x1, Pallas kernels, halo_features(): pl.pallas_call(functools.partial(halo_features_kernel, block_total, own_b...  0.84 us
  transfers between devices with their start and end apart: 7, of which 4 were waited for; matrix products, arithmetic and copies ran while one was open for 0% of the time, Pallas kernels for 38%

profile of v1, /device:TPU:0, one launch (start us, length us, event | category | flops | bytes accessed | tf_op | source)
XLA Modules:
  0.0 28.9 jit_solution(9102664066306934953)
XLA Ops:
  0.0 0.5 %collective-permute-start = (f32[2,32768]{1,0:T(2,128)}, f32[2,32768]{1,0:T(2,128)S(1)}, u32[]{:S(2)}, u32[]{:S(2)}) collective-permute-start(f32[2,32768]{1,0:T(2,128)} %bitcast.18), channel_id=1, source_target_pairs={{1,0},{0,1},{3,2},{2,3},{5,4},{4,5},{7,6},{6,7},{9,8},{8,9},{11,10... | collective-permute-start | bytes 786440 | tf_op jit(solution)/shard_map/ppermute | solution.py:60
  0.5 1.5 %prepare.1 = (f32[3,32768]{1,0:T(4,128)S(1)}, f32[256,128]{1,0:T(8,128)S(1)}, f32[2,16384]{1,0:T(2,128)S(1)}, s32[8,128]{1,0:T(8,128)S(1)}, f32[208,128]{1,0:T(8,128)S(1)}, /*index=5*/f32[208,128]{1,0:T(8,128)S(1)}) custom-call(s32[1]{0:T(128)} %bitcast.event_ref.refs_0_, s32[1]{0:T(128)} %bitcast.1.cut_ref, s32[1,4]{1,0:T(1,128)} %bitcast.22, ...), custom_call_target="tpu_custom_call" | custom-call | flops 2300000000 | bytes 1000000 | tf_op jit(solution)/shard_map/prepare/pallas_call | solution.py:276
  2.0 0.0 collective-permute-done.near_ref
  2.0 4.9 %collective-permute-start.1 = (f32[208,128]{1,0:T(8,128)S(1)}, f32[208,128]{1,0:T(8,128)S(1)}, u32[]{:S(2)}, u32[]{:S(2)}) collective-permute-start(f32[208,128]{1,0:T(8,128)S(1)} %get-tuple-element.32), channel_id=1, source_target_pairs={{0,12},{4,8},{8,4},{12,0},{1,13},{5,9},{9,5},{13,1},{2,14},{6,10},... | collective-permute-start | bytes 319496 | tf_op jit(solution)/shard_map/ppermute | solution.py:55
  6.9 0.0 collective-permute-start.2
  6.9 1.5 %collective-permute-start.3 = (f32[2,16384]{1,0:T(2,128)S(1)}, f32[2,16384]{1,0:T(2,128)S(1)}, u32[]{:S(2)}, u32[]{:S(2)}) collective-permute-start(f32[2,16384]{1,0:T(2,128)S(1)} %get-tuple-element.37.first_ref), channel_id=1, source_target_pairs={{2,0},{3,1},{0,2},{1,3},{6,4},{7,5},{4,6},{5,7},{10,8},{11,9},{8,1... | collective-permute-start | bytes 393224 | tf_op jit(solution)/shard_map/ppermute | solution.py:60
  8.4 0.0 copy-start
  8.4 4.0 %own_features.1 = (bf16[257,128,48]{2,1,0:T(8,128)(2,1)S(1)}, bf16[64,48,128]{2,1,0:T(8,128)(2,1)S(1)}, f32[8,128]{1,0:T(8,128)S(1)}) custom-call(s32[1]{0:T(128)} %bitcast.event_ref.refs_0_, f32[3,32768]{1,0:T(4,128)S(1)} %get-tuple-element.26.coords_ref, f32[256,128]{1,0:T(8,128)S(1)} %get-tuple-element.27.volume_ref), custom_call_target="tpu_custom_call" | custom-call | flops 4600000000 | bytes 1000000 | tf_op jit(solution)/shard_map/own_features/pallas_call | solution.py:122
  12.3 0.0 collective-permute-done.3.second_ref
  12.4 0.1 collective-permute-start.4
  12.5 0.0 collective-permute-done.1.refs_0_
  12.5 0.2 collective-permute-done.2.refs_1_
  12.7 0.0 copy-done
  12.7 0.8 %halo_features.1 = (bf16[192,48,128]{2,1,0:T(8,128)(2,1)S(1)}, s32[3,8,128]{2,1,0:T(8,128)S(4)}) custom-call(s32[8,128]{1,0:T(8,128)S(1)} %get-tuple-element.25.own_ref, bf16[64,48,128]{2,1,0:T(8,128)(2,1)S(1)} %get-tuple-element.28.near_ref, s32[4,64]{1,0:T(4,128)S(1)} %bitcast.17, f32[208,128]{1,0:T(8,128)S(1)} %collective-permute-done.1.refs_0_, ...), custom_call_target="tpu_custom_call" | custom-call | flops 1150000000 | bytes 1000000 | tf_op jit(solution)/shard_map/halo_features/pallas_call | solution.py:345
  13.6 0.2 collective-permute-done.4.refs_2_
  13.8 6.5 %first_totals.1 = (f32[3,64,128]{2,1,0:T(8,128)S(1)}, f32[3,64,128]{2,1,0:T(8,128)S(1)}, f32[512,128]{1,0:T(8,128)S(1)}, bf16[257,8,256]{2,1,0:T(8,128)(2,1)S(1)}, f32[32,128,256]{2,1,0:T(8,128)S(1)}) custom-call(s32[3,8,128]{2,1,0:T(8,128)S(4)} %get-tuple-element.34.list_ref, bf16[257,128,48]{2,1,0:T(8,128)(2,1)S(1)} %get-tuple-element.35.source_ref, ...), custom_call_target="tpu_custom_call" | custom-call | flops 9200000000 | bytes 1000000 | tf_op jit(solution)/shard_map/first_totals/pallas_call | solution.py:533
  20.3 1.7 %collective-permute-start.5 = (f32[3,64,128]{2,1,0:T(8,128)S(1)}, f32[3,64,128]{2,1,0:T(8,128)S(1)}, u32[]{:S(2)}, u32[]{:S(2)}) collective-permute-start(f32[3,64,128]{2,1,0:T(8,128)S(1)} %get-tuple-element.43), channel_id=1, source_target_pairs={{0,12},{4,8},{8,4},{12,0},{1,13},{5,9},{9,5},{13,1},{2,14},{6,10},... | collective-permute-start | bytes 294920 | tf_op jit(solution)/shard_map/ppermute | solution.py:55
  21.9 0.5 %collective-permute-start.6 = (f32[3,64,128]{2,1,0:T(8,128)S(1)}, f32[3,64,128]{2,1,0:T(8,128)S(1)}, u32[]{:S(2)}, u32[]{:S(2)}) collective-permute-start(f32[3,64,128]{2,1,0:T(8,128)S(1)} %get-tuple-element.44), channel_id=1, source_target_pairs={{0,4},{4,0},{8,12},{12,8},{1,5},{5,1},{9,13},{13,9},{2,6},{6,2},{1... | collective-permute-start | bytes 294920 | tf_op jit(solution)/shard_map/ppermute | solution.py:55
  22.4 4.5 %last_totals.1 = (f32[3,64,128]{2,1,0:T(8,128)S(1)}, f32[32,128,256]{2,1,0:T(8,128)S(1)}) custom-call(s32[3,8,128]{2,1,0:T(8,128)S(4)} %get-tuple-element.34.list_ref, bf16[257,128,48]{2,1,0:T(8,128)(2,1)S(1)} %get-tuple-element.35.source_ref, bf16[192,48,128]{2,1,0:T(8,128)(2,1)S(1)} %get-tuple-element.36.target_ref, ...), custom_call_target="tpu_custom_call", output_to_operand_aliasing={{1}: (5, {})} | custom-call | flops 9200000000 | bytes 1000000 | tf_op jit(solution)/shard_map/last_totals/pallas_call | solution.py:568
  27.0 0.8 %collective-permute-done.5 = f32[3,64,128]{2,1,0:T(8,128)S(1)} collective-permute-done((f32[3,64,128]{2,1,0:T(8,128)S(1)}, f32[3,64,128]{2,1,0:T(8,128)S(1)}, u32[]{:S(2)}, u32[]{:S(2)}) %collective-permute-start.5) | collective-permute-done | bytes 98336 | tf_op jit(solution)/shard_map/ppermute | solution.py:55
  27.8 0.3 %collective-permute-done.6 = f32[3,64,128]{2,1,0:T(8,128)S(1)} collective-permute-done((f32[3,64,128]{2,1,0:T(8,128)S(1)}, f32[3,64,128]{2,1,0:T(8,128)S(1)}, u32[]{:S(2)}, u32[]{:S(2)}) %collective-permute-start.6) | collective-permute-done | bytes 98336 | tf_op jit(solution)/shard_map/ppermute | solution.py:55
  28.2 0.7 %copy.11 = f32[1,2,64,128]{3,1,2,0:T(2,128)} copy(f32[1,2,64,128]{3,2,1,0:T(8,128)S(1)} %fusion) | data formatting | bytes 131072
  (5 shorter events, 0.1 us)
Async XLA Ops:
  0.0 2.0 %collective-permute-start = (f32[2,32768]{1,0:T(2,128)}, f32[2,32768]{1,0:T(2,128)S(1)}, u32[]{:S(2)}, u32[]{:S(2)}) collective-permute-start(f32[2,32768]{1,0:T(2,128)} %bitcast.18), channel_id=1, source_target_pairs={{1,0},{0,1},{3,2},{2,3},{5,4},{4,5},{7,6},{6,7},{9,8},{8,9},{11,10... | collective-permute-start | bytes 786440 | tf_op jit(solution)/shard_map/ppermute | solution.py:60
  2.0 10.4 %collective-permute-start.1 = (f32[208,128]{1,0:T(8,128)S(1)}, f32[208,128]{1,0:T(8,128)S(1)}, u32[]{:S(2)}, u32[]{:S(2)}) collective-permute-start(f32[208,128]{1,0:T(8,128)S(1)} %get-tuple-element.32), channel_id=1, source_target_pairs={{0,12},{4,8},{8,4},{12,0},{1,13},{5,9},{9,5},{13,1},{2,14},{6,10},... | collective-permute-start | bytes 319496 | tf_op jit(solution)/shard_map/ppermute | solution.py:55
  6.9 5.8 %collective-permute-start.2 = (f32[208,128]{1,0:T(8,128)S(1)}, f32[208,128]{1,0:T(8,128)S(1)}, u32[]{:S(2)}, u32[]{:S(2)}) collective-permute-start(f32[208,128]{1,0:T(8,128)S(1)} %get-tuple-element.33), channel_id=1, source_target_pairs={{0,4},{4,0},{8,12},{12,8},{1,5},{5,1},{9,13},{13,9},{2,6},{6,2},{1... | collective-permute-start | bytes 319496 | tf_op jit(solution)/shard_map/ppermute | solution.py:55
  6.9 5.5 %collective-permute-start.3 = (f32[2,16384]{1,0:T(2,128)S(1)}, f32[2,16384]{1,0:T(2,128)S(1)}, u32[]{:S(2)}, u32[]{:S(2)}) collective-permute-start(f32[2,16384]{1,0:T(2,128)S(1)} %get-tuple-element.37.first_ref), channel_id=1, source_target_pairs={{2,0},{3,1},{0,2},{1,3},{6,4},{7,5},{4,6},{5,7},{10,8},{11,9},{8,1... | collective-permute-start | bytes 393224 | tf_op jit(solution)/shard_map/ppermute | solution.py:60
  8.4 4.3 %copy-start = (s32[1,1,4,64]{3,2,1,0:T(4,128)S(1)}, s32[1,1,4,64]{3,2,1,0:T(4,128)}, u32[]{:S(2)}) copy-start(s32[1,1,4,64]{3,2,1,0:T(4,128)} %param.10) | copy-start | bytes 3076
  12.4 1.4 %collective-permute-start.4 = (f32[2,16384]{1,0:T(2,128)S(1)}, f32[2,16384]{1,0:T(2,128)S(1)}, u32[]{:S(2)}, u32[]{:S(2)}) collective-permute-start(f32[2,16384]{1,0:T(2,128)S(1)} %added.1.refs_1_), channel_id=1, source_target_pairs={{1,0},{0,1},{3,2},{2,3},{5,4},{4,5},{7,6},{6,7},{9,8},{8,9},{11,10... | collective-permute-start | bytes 393224 | tf_op jit(solution)/shard_map/ppermute | solution.py:60
  20.3 7.6 %collective-permute-start.5 = (f32[3,64,128]{2,1,0:T(8,128)S(1)}, f32[3,64,128]{2,1,0:T(8,128)S(1)}, u32[]{:S(2)}, u32[]{:S(2)}) collective-permute-start(f32[3,64,128]{2,1,0:T(8,128)S(1)} %get-tuple-element.43), channel_id=1, source_target_pairs={{0,12},{4,8},{8,4},{12,0},{1,13},{5,9},{9,5},{13,1},{2,14},{6,10},... | collective-permute-start | bytes 294920 | tf_op jit(solution)/shard_map/ppermute | solution.py:55
  21.9 6.2 %collective-permute-start.6 = (f32[3,64,128]{2,1,0:T(8,128)S(1)}, f32[3,64,128]{2,1,0:T(8,128)S(1)}, u32[]{:S(2)}, u32[]{:S(2)}) collective-permute-start(f32[3,64,128]{2,1,0:T(8,128)S(1)} %get-tuple-element.44), channel_id=1, source_target_pairs={{0,4},{4,0},{8,12},{12,8},{1,5},{5,1},{9,13},{13,9},{2,6},{6,2},{1... | collective-permute-start | bytes 294920 | tf_op jit(solution)/shard_map/ppermute | solution.py:55

commit v2 on v1

--- a/solution.py
+++ b/solution.py
@@ -12,6 +12,7 @@
 FEATURES = 48
 STEP_BITS = 5
 STEP = 1 << STEP_BITS
+SLOTS = 32
 QUOTA = 6
 FIELD = 10
 sigma_km = 50.0
@@ -73,11 +74,12 @@
     return jnp.where(row < 3, offsets, rows)
 
 
-def place(coords_ref, pad_ref, slot, b):
+def place(coords_ref, b):
     at = pl.ds(pl.multiple_of(b * BLOCK, BLOCK), BLOCK)
-    pad_ref[slot, 0:3, :] = (coords_ref[:, at] - centre_km) * scale
-    offsets = pad_ref[slot]
-    return offsets, -0.5 * jnp.sum(offsets * offsets, axis=0, keepdims=True)
+    offsets = (coords_ref[:, at] - centre_km) * scale
+    squares = offsets * offsets
+    norm = -0.5 * (squares[0:1] + squares[1:2] + squares[2:3])
+    return jnp.concatenate([offsets, jnp.zeros((5, BLOCK), f32)], axis=0), norm
 
 
 def target_features(offsets, norm):
@@ -86,18 +88,17 @@
 
 
 def own_features_kernel(
-    event_ref, coords_ref, volume_ref, source_ref, target_ref, mark_ref, pad_ref, log_ref
+    event_ref, coords_ref, volume_ref, source_ref, target_ref, mark_ref, log_ref
 ):
     block_total = volume_ref.shape[0]
     own_blocks = target_ref.shape[0]
-    slots = pad_ref.shape[0]
-    pad_ref[...] = jnp.zeros(pad_ref.shape, f32)
+    slots = SLOTS
     log_ref[...] = jnp.log2(volume_ref[...])
 
     def some_sources(n, _):
         for slot in range(slots):
             b = n * slots + slot
-            offsets, norm = place(coords_ref, pad_ref, slot, b)
+            offsets, norm = place(coords_ref, b)
             high, middle, low = split(feature_rows(offsets, norm + log_ref[pl.ds(b, 1), :], 1.0))
             rows = jnp.concatenate([high, high, high, middle, middle, low], axis=0)
             source_ref[b] = rows.astype(bf16).T
@@ -107,7 +108,7 @@
         for slot in range(slots):
             t = n * slots + slot
             block = event_ref[0] * own_blocks + t
-            target_ref[t] = target_features(*place(coords_ref, pad_ref, slot, block))
+            target_ref[t] = target_features(*place(coords_ref, block))
         return 0
 
     lax.fori_loop(0, block_total // slots, some_sources, 0)
@@ -128,10 +129,7 @@
         ),
         in_specs=[smem(), vmem(), vmem()],
         out_specs=(vmem(),) * 3,
-        scratch_shapes=[
-            pltpu.VMEM((16, 8, BLOCK), f32),
-            pltpu.VMEM((block_total, BLOCK), f32),
-        ],
+        scratch_shapes=[pltpu.VMEM((block_total, BLOCK), f32)],
         compiler_params=params(8),
         cost_estimate=lasting(4),
         name="own_features",
@@ -352,7 +350,7 @@
         out_specs=(vmem(), smem()),
         scratch_shapes=[
             pltpu.VMEM(lists, i32),
-            pltpu.VMEM((16, 8, BLOCK), f32),
+            pltpu.VMEM((SLOTS, 8, BLOCK), f32),
             pltpu.VMEM((8, BLOCK), i32),
             pltpu.SemaphoreType.DMA,
         ],

time: 29.3 us -> 29 us (0.990)
    pallas_call x1, Pallas kernels: 4.54 us -> 5.45 us  [last_totals(): pl.pallas_call(functools.partial(last_totals_kernel, own_blocks), out_sha...]
    pallas_call x1, Pallas kernels: 3.95 us -> 3.15 us  [own_features(): pl.pallas_call(own_features_kernel, out_shape=(pltpu.VMEM((block_total +...]
    ppermute x3, waiting for transfers between devices: 0.24 us -> 0.95 us  [crossed(): return lax.ppermute(block, axis, route)]
    ppermute x4, waiting for transfers between devices: 1.39 us -> 0.8 us  [swapped(): return lax.ppermute(block, 'cuts', route)]
  transfers between devices with their start and end apart: 7 -> 7, of which waited for: 4 -> 5; matrix products, arithmetic and copies ran while one was open for 0% -> 0% of each run, Pallas kernels for 38% -> 38%
where the time goes in v2:
time: 29 us; the launch traced here: 28.8 us
  Pallas kernels  17.5 us (60%)
  starting transfers between devices  8.79 us (30%)
  waiting for transfers between devices  1.75 us (6%)
  local copies, waits for them, and re-layouts  0.69 us (2%)
    ppermute x4, starting transfers between devices, swapped(): return lax.ppermute(block, 'cuts', route)  6.78 us
    pallas_call x1, Pallas kernels, first_totals(): pl.pallas_call(functools.partial(first_totals_kernel, own_blocks), out_sh...  6.45 us
    pallas_call x1, Pallas kernels, last_totals(): pl.pallas_call(functools.partial(last_totals_kernel, own_blocks), out_sha...  5.45 us
    pallas_call x1, Pallas kernels, own_features(): pl.pallas_call(own_features_kernel, out_shape=(pltpu.VMEM((block_total +...  3.15 us
    ppermute x3, starting transfers between devices, crossed(): return lax.ppermute(block, axis, route)  2.01 us
    pallas_call x1, Pallas kernels, prepare(): pl.pallas_call(functools.partial(prepare_kernel, strides, capacity), out_...  1.51 us
    ppermute x3, waiting for transfers between devices, crossed(): return lax.ppermute(block, axis, route)  0.95 us
    pallas_call x1, Pallas kernels, halo_features(): pl.pallas_call(functools.partial(halo_features_kernel, block_total, own_b...  0.84 us
  transfers between devices with their start and end apart: 7, of which 5 were waited for; matrix products, arithmetic and copies ran while one was open for 0% of the time, Pallas kernels for 38%

profile of v2, /device:TPU:0, one launch (start us, length us, event | category | flops | bytes accessed | tf_op | source)
XLA Modules:
  0.0 28.8 jit_solution(12087845947853800528)
XLA Ops:
  0.0 0.5 %collective-permute-start = (f32[2,32768]{1,0:T(2,128)}, f32[2,32768]{1,0:T(2,128)S(1)}, u32[]{:S(2)}, u32[]{:S(2)}) collective-permute-start(f32[2,32768]{1,0:T(2,128)} %bitcast.18), channel_id=1, source_target_pairs={{1,0},{0,1},{3,2},{2,3},{5,4},{4,5},{7,6},{6,7},{9,8},{8,9},{11,10... | collective-permute-start | bytes 786440 | tf_op jit(solution)/shard_map/ppermute | solution.py:61
  0.5 1.5 %prepare.1 = (f32[3,32768]{1,0:T(4,128)S(1)}, f32[256,128]{1,0:T(8,128)S(1)}, f32[2,16384]{1,0:T(2,128)S(1)}, s32[8,128]{1,0:T(8,128)S(1)}, f32[208,128]{1,0:T(8,128)S(1)}, /*index=5*/f32[208,128]{1,0:T(8,128)S(1)}) custom-call(s32[1]{0:T(128)} %bitcast.event_ref.refs_0_, s32[1]{0:T(128)} %bitcast.1.cut_ref, s32[1,4]{1,0:T(1,128)} %bitcast.22, ...), custom_call_target="tpu_custom_call" | custom-call | flops 2300000000 | bytes 1000000 | tf_op jit(solution)/shard_map/prepare/pallas_call | solution.py:274
  2.0 0.0 collective-permute-done.near_ref
  2.0 4.9 %collective-permute-start.1 = (f32[208,128]{1,0:T(8,128)S(1)}, f32[208,128]{1,0:T(8,128)S(1)}, u32[]{:S(2)}, u32[]{:S(2)}) collective-permute-start(f32[208,128]{1,0:T(8,128)S(1)} %get-tuple-element.32), channel_id=1, source_target_pairs={{0,12},{4,8},{8,4},{12,0},{1,13},{5,9},{9,5},{13,1},{2,14},{6,10},... | collective-permute-start | bytes 319496 | tf_op jit(solution)/shard_map/ppermute | solution.py:56
  6.9 0.0 collective-permute-start.2
  6.9 1.5 %collective-permute-start.3 = (f32[2,16384]{1,0:T(2,128)S(1)}, f32[2,16384]{1,0:T(2,128)S(1)}, u32[]{:S(2)}, u32[]{:S(2)}) collective-permute-start(f32[2,16384]{1,0:T(2,128)S(1)} %get-tuple-element.37.first_ref), channel_id=1, source_target_pairs={{2,0},{3,1},{0,2},{1,3},{6,4},{7,5},{4,6},{5,7},{10,8},{11,9},{8,1... | collective-permute-start | bytes 393224 | tf_op jit(solution)/shard_map/ppermute | solution.py:61
  8.4 0.0 copy-start
  8.4 3.2 %own_features.1 = (bf16[257,128,48]{2,1,0:T(8,128)(2,1)S(1)}, bf16[64,48,128]{2,1,0:T(8,128)(2,1)S(1)}, f32[8,128]{1,0:T(8,128)S(1)}) custom-call(s32[1]{0:T(128)} %bitcast.event_ref.refs_0_, f32[3,32768]{1,0:T(4,128)S(1)} %get-tuple-element.26.coords_ref, f32[256,128]{1,0:T(8,128)S(1)} %get-tuple-element.27.volume_ref), custom_call_target="tpu_custom_call" | custom-call | flops 4600000000 | bytes 1000000 | tf_op jit(solution)/shard_map/own_features/pallas_call | solution.py:123
  11.6 0.8 %collective-permute-done.3.second_ref = f32[2,16384]{1,0:T(2,128)S(1)} collective-permute-done((f32[2,16384]{1,0:T(2,128)S(1)}, f32[2,16384]{1,0:T(2,128)S(1)}, u32[]{:S(2)}, u32[]{:S(2)}) %collective-permute-start.3) | collective-permute-done | bytes 131104 | tf_op jit(solution)/shard_map/ppermute | solution.py:61
  12.3 0.1 collective-permute-start.4
  12.4 0.0 collective-permute-done.1.refs_0_
  12.4 0.3 collective-permute-done.2.refs_1_
  12.7 0.0 copy-done
  12.7 0.8 %halo_features.1 = (bf16[192,48,128]{2,1,0:T(8,128)(2,1)S(1)}, s32[3,8,128]{2,1,0:T(8,128)S(4)}) custom-call(s32[8,128]{1,0:T(8,128)S(1)} %get-tuple-element.25.own_ref, bf16[64,48,128]{2,1,0:T(8,128)(2,1)S(1)} %get-tuple-element.28.near_ref, s32[4,64]{1,0:T(4,128)S(1)} %bitcast.17, f32[208,128]{1,0:T(8,128)S(1)} %collective-permute-done.1.refs_0_, ...), custom_call_target="tpu_custom_call" | custom-call | flops 1150000000 | bytes 1000000 | tf_op jit(solution)/shard_map/halo_features/pallas_call | solution.py:343
  13.6 0.2 collective-permute-done.4.refs_2_
  13.7 6.5 %first_totals.1 = (f32[3,64,128]{2,1,0:T(8,128)S(1)}, f32[3,64,128]{2,1,0:T(8,128)S(1)}, f32[512,128]{1,0:T(8,128)S(1)}, bf16[257,8,256]{2,1,0:T(8,128)(2,1)S(1)}, f32[32,128,256]{2,1,0:T(8,128)S(1)}) custom-call(s32[3,8,128]{2,1,0:T(8,128)S(4)} %get-tuple-element.34.list_ref, bf16[257,128,48]{2,1,0:T(8,128)(2,1)S(1)} %get-tuple-element.35.source_ref, ...), custom_call_target="tpu_custom_call" | custom-call | flops 9200000000 | bytes 1000000 | tf_op jit(solution)/shard_map/first_totals/pallas_call | solution.py:531
  20.2 1.7 %collective-permute-start.5 = (f32[3,64,128]{2,1,0:T(8,128)S(1)}, f32[3,64,128]{2,1,0:T(8,128)S(1)}, u32[]{:S(2)}, u32[]{:S(2)}) collective-permute-start(f32[3,64,128]{2,1,0:T(8,128)S(1)} %get-tuple-element.43), channel_id=1, source_target_pairs={{0,12},{4,8},{8,4},{12,0},{1,13},{5,9},{9,5},{13,1},{2,14},{6,10},... | collective-permute-start | bytes 294920 | tf_op jit(solution)/shard_map/ppermute | solution.py:56
  21.9 0.2 collective-permute-start.6
  22.1 5.5 %last_totals.1 = (f32[3,64,128]{2,1,0:T(8,128)S(1)}, f32[32,128,256]{2,1,0:T(8,128)S(1)}) custom-call(s32[3,8,128]{2,1,0:T(8,128)S(4)} %get-tuple-element.34.list_ref, bf16[257,128,48]{2,1,0:T(8,128)(2,1)S(1)} %get-tuple-element.35.source_ref, bf16[192,48,128]{2,1,0:T(8,128)(2,1)S(1)} %get-tuple-element.36.target_ref, ...), custom_call_target="tpu_custom_call", output_to_operand_aliasing={{1}: (5, {})} | custom-call | flops 9200000000 | bytes 1000000 | tf_op jit(solution)/shard_map/last_totals/pallas_call | solution.py:566
  27.6 0.2 collective-permute-done.5
  27.8 0.3 %collective-permute-done.6 = f32[3,64,128]{2,1,0:T(8,128)S(1)} collective-permute-done((f32[3,64,128]{2,1,0:T(8,128)S(1)}, f32[3,64,128]{2,1,0:T(8,128)S(1)}, u32[]{:S(2)}, u32[]{:S(2)}) %collective-permute-start.6) | collective-permute-done | bytes 98336 | tf_op jit(solution)/shard_map/ppermute | solution.py:56
  28.1 0.7 %copy.11 = f32[1,2,64,128]{3,1,2,0:T(2,128)} copy(f32[1,2,64,128]{3,2,1,0:T(8,128)S(1)} %fusion) | data formatting | bytes 131072
  (5 shorter events, 0.1 us)
Async XLA Ops:
  0.0 2.0 %collective-permute-start = (f32[2,32768]{1,0:T(2,128)}, f32[2,32768]{1,0:T(2,128)S(1)}, u32[]{:S(2)}, u32[]{:S(2)}) collective-permute-start(f32[2,32768]{1,0:T(2,128)} %bitcast.18), channel_id=1, source_target_pairs={{1,0},{0,1},{3,2},{2,3},{5,4},{4,5},{7,6},{6,7},{9,8},{8,9},{11,10... | collective-permute-start | bytes 786440 | tf_op jit(solution)/shard_map/ppermute | solution.py:61
  2.0 10.4 %collective-permute-start.1 = (f32[208,128]{1,0:T(8,128)S(1)}, f32[208,128]{1,0:T(8,128)S(1)}, u32[]{:S(2)}, u32[]{:S(2)}) collective-permute-start(f32[208,128]{1,0:T(8,128)S(1)} %get-tuple-element.32), channel_id=1, source_target_pairs={{0,12},{4,8},{8,4},{12,0},{1,13},{5,9},{9,5},{13,1},{2,14},{6,10},... | collective-permute-start | bytes 319496 | tf_op jit(solution)/shard_map/ppermute | solution.py:56
  6.9 5.8 %collective-permute-start.2 = (f32[208,128]{1,0:T(8,128)S(1)}, f32[208,128]{1,0:T(8,128)S(1)}, u32[]{:S(2)}, u32[]{:S(2)}) collective-permute-start(f32[208,128]{1,0:T(8,128)S(1)} %get-tuple-element.33), channel_id=1, source_target_pairs={{0,4},{4,0},{8,12},{12,8},{1,5},{5,1},{9,13},{13,9},{2,6},{6,2},{1... | collective-permute-start | bytes 319496 | tf_op jit(solution)/shard_map/ppermute | solution.py:56
  6.9 5.4 %collective-permute-start.3 = (f32[2,16384]{1,0:T(2,128)S(1)}, f32[2,16384]{1,0:T(2,128)S(1)}, u32[]{:S(2)}, u32[]{:S(2)}) collective-permute-start(f32[2,16384]{1,0:T(2,128)S(1)} %get-tuple-element.37.first_ref), channel_id=1, source_target_pairs={{2,0},{3,1},{0,2},{1,3},{6,4},{7,5},{4,6},{5,7},{10,8},{11,9},{8,1... | collective-permute-start | bytes 393224 | tf_op jit(solution)/shard_map/ppermute | solution.py:61
  8.4 4.3 %copy-start = (s32[1,1,4,64]{3,2,1,0:T(4,128)S(1)}, s32[1,1,4,64]{3,2,1,0:T(4,128)}, u32[]{:S(2)}) copy-start(s32[1,1,4,64]{3,2,1,0:T(4,128)} %param.10) | copy-start | bytes 3076
  12.3 1.4 %collective-permute-start.4 = (f32[2,16384]{1,0:T(2,128)S(1)}, f32[2,16384]{1,0:T(2,128)S(1)}, u32[]{:S(2)}, u32[]{:S(2)}) collective-permute-start(f32[2,16384]{1,0:T(2,128)S(1)} %added.1.refs_1_), channel_id=1, source_target_pairs={{1,0},{0,1},{3,2},{2,3},{5,4},{4,5},{7,6},{6,7},{9,8},{8,9},{11,10... | collective-permute-start | bytes 393224 | tf_op jit(solution)/shard_map/ppermute | solution.py:61
  20.2 7.5 %collective-permute-start.5 = (f32[3,64,128]{2,1,0:T(8,128)S(1)}, f32[3,64,128]{2,1,0:T(8,128)S(1)}, u32[]{:S(2)}, u32[]{:S(2)}) collective-permute-start(f32[3,64,128]{2,1,0:T(8,128)S(1)} %get-tuple-element.43), channel_id=1, source_target_pairs={{0,12},{4,8},{8,4},{12,0},{1,13},{5,9},{9,5},{13,1},{2,14},{6,10},... | collective-permute-start | bytes 294920 | tf_op jit(solution)/shard_map/ppermute | solution.py:56
  21.9 6.1 %collective-permute-start.6 = (f32[3,64,128]{2,1,0:T(8,128)S(1)}, f32[3,64,128]{2,1,0:T(8,128)S(1)}, u32[]{:S(2)}, u32[]{:S(2)}) collective-permute-start(f32[3,64,128]{2,1,0:T(8,128)S(1)} %get-tuple-element.44), channel_id=1, source_target_pairs={{0,4},{4,0},{8,12},{12,8},{1,5},{5,1},{9,13},{13,9},{2,6},{6,2},{1... | collective-permute-start | bytes 294920 | tf_op jit(solution)/shard_map/ppermute | solution.py:56

commit v3 on v2

--- a/solution.py
+++ b/solution.py
@@ -583,6 +583,27 @@
     return total
 
 
+def smoothed_kernel(*refs):
+    *parts, out_ref = refs
+    totals = [sum(part[r] for part in parts) for r in range(3)]
+    for k in range(2):
+        ratio = totals[k + 1] / totals[0]
+        for t in range(ratio.shape[0]):
+            out_ref[k : k + 1, t * BLOCK : (t + 1) * BLOCK] = ratio[t : t + 1]
+
+
+def smoothed(parts):
+    return pl.pallas_call(
+        smoothed_kernel,
+        out_shape=jax.ShapeDtypeStruct((2, parts[0].shape[1] * BLOCK), f32),
+        in_specs=[vmem()] * len(parts),
+        out_specs=vmem(),
+        compiler_params=params(4),
+        cost_estimate=lasting(0.2),
+        name="smoothed",
+    )(*parts)
+
+
 def local(partials, coords, volume, send_blocks, halo_counts, source_slots, source_counts):
     cut_count = lax.axis_size("cuts")
     event_count = lax.axis_size("event")
@@ -623,9 +644,7 @@
     )
     returned = [swapped(t, *turn) for t, turn in zip(halo_totals, turns)]
     totals = last_totals(lists, sources, targets, values, own_sum, exponent)
-    for part in returned:
-        totals = totals + part
-    return (totals[1:3] / totals[0]).reshape(2, own_blocks * BLOCK)
+    return smoothed([totals, *returned])
 
 
 def solution(mesh):

time: 29 us -> 29.3 us (1.010)
  Pallas kernels: 17.5 us -> 19 us
  local copies, waits for them, and re-layouts: 0.69 us -> 0.01 us
  waiting for transfers between devices: 1.75 us -> 1.24 us
    pallas_call x1, Pallas kernels: 5.45 us -> 6.35 us  [last_totals(): pl.pallas_call(functools.partial(last_totals_kernel, own_blocks), out_sha...]
    unnamed x3 -> x2, local copies, waits for them, and re-layouts: 0.69 us -> 0.01 us
    pallas_call x0 -> x1, Pallas kernels: none -> 0.68 us  [smoothed(): pl.pallas_call(smoothed_kernel, out_shape=jax.ShapeDtypeStruct((2, parts[...]
    ppermute x4, waiting for transfers between devices: 0.8 us -> 0.29 us  [swapped(): return lax.ppermute(block, 'cuts', route)]
  transfers between devices with their start and end apart: 7 -> 7, of which waited for: 5 -> 3; matrix products, arithmetic and copies ran while one was open for 0% -> 0% of each run, Pallas kernels for 38% -> 41%
where the time goes in v3:
time: 29.3 us; the launch traced here: 29.2 us
  Pallas kernels  19 us (65%)
  starting transfers between devices  8.78 us (30%)
  waiting for transfers between devices  1.24 us (4%)
    ppermute x4, starting transfers between devices, swapped(): return lax.ppermute(block, 'cuts', route)  6.77 us
    pallas_call x1, Pallas kernels, first_totals(): pl.pallas_call(functools.partial(first_totals_kernel, own_blocks), out_sh...  6.46 us
    pallas_call x1, Pallas kernels, last_totals(): pl.pallas_call(functools.partial(last_totals_kernel, own_blocks), out_sha...  6.35 us
    pallas_call x1, Pallas kernels, own_features(): pl.pallas_call(own_features_kernel, out_shape=(pltpu.VMEM((block_total +...  3.15 us
    ppermute x3, starting transfers between devices, crossed(): return lax.ppermute(block, axis, route)  2.01 us
    pallas_call x1, Pallas kernels, prepare(): pl.pallas_call(functools.partial(prepare_kernel, strides, capacity), out_...  1.51 us
    ppermute x3, waiting for transfers between devices, crossed(): return lax.ppermute(block, axis, route)  0.95 us
    pallas_call x1, Pallas kernels, halo_features(): pl.pallas_call(functools.partial(halo_features_kernel, block_total, own_b...  0.84 us
  transfers between devices with their start and end apart: 7, of which 3 were waited for; matrix products, arithmetic and copies ran while one was open for 0% of the time, Pallas kernels for 41%

profile of v3, /device:TPU:0, one launch (start us, length us, event | category | flops | bytes accessed | tf_op | source)
XLA Modules:
  0.0 29.2 jit_solution(6868792081802326902)
XLA Ops:
  0.0 0.5 %collective-permute-start = (f32[2,32768]{1,0:T(2,128)}, f32[2,32768]{1,0:T(2,128)S(1)}, u32[]{:S(2)}, u32[]{:S(2)}) collective-permute-start(f32[2,32768]{1,0:T(2,128)} %bitcast.11), channel_id=1, source_target_pairs={{1,0},{0,1},{3,2},{2,3},{5,4},{4,5},{7,6},{6,7},{9,8},{8,9},{11,10... | collective-permute-start | bytes 786440 | tf_op jit(solution)/shard_map/ppermute | solution.py:61
  0.5 1.5 %prepare.1 = (f32[3,32768]{1,0:T(4,128)S(1)}, f32[256,128]{1,0:T(8,128)S(1)}, f32[2,16384]{1,0:T(2,128)S(1)}, s32[8,128]{1,0:T(8,128)S(1)}, f32[208,128]{1,0:T(8,128)S(1)}, /*index=5*/f32[208,128]{1,0:T(8,128)S(1)}) custom-call(s32[1]{0:T(128)} %bitcast.event_ref.refs_0_, s32[1]{0:T(128)} %bitcast.1.cut_ref, s32[1,4]{1,0:T(1,128)} %bitcast.15, ...), custom_call_target="tpu_custom_call" | custom-call | flops 2300000000 | bytes 1000000 | tf_op jit(solution)/shard_map/prepare/pallas_call | solution.py:274
  2.0 0.0 collective-permute-done.near_ref
  2.0 4.9 %collective-permute-start.1 = (f32[208,128]{1,0:T(8,128)S(1)}, f32[208,128]{1,0:T(8,128)S(1)}, u32[]{:S(2)}, u32[]{:S(2)}) collective-permute-start(f32[208,128]{1,0:T(8,128)S(1)} %get-tuple-element.32), channel_id=1, source_target_pairs={{0,12},{4,8},{8,4},{12,0},{1,13},{5,9},{9,5},{13,1},{2,14},{6,10},... | collective-permute-start | bytes 319496 | tf_op jit(solution)/shard_map/ppermute | solution.py:56
  6.9 0.0 collective-permute-start.2
  6.9 1.5 %collective-permute-start.3 = (f32[2,16384]{1,0:T(2,128)S(1)}, f32[2,16384]{1,0:T(2,128)S(1)}, u32[]{:S(2)}, u32[]{:S(2)}) collective-permute-start(f32[2,16384]{1,0:T(2,128)S(1)} %get-tuple-element.37.first_ref), channel_id=1, source_target_pairs={{2,0},{3,1},{0,2},{1,3},{6,4},{7,5},{4,6},{5,7},{10,8},{11,9},{8,1... | collective-permute-start | bytes 393224 | tf_op jit(solution)/shard_map/ppermute | solution.py:61
  8.4 0.0 copy-start
  8.4 3.2 %own_features.1 = (bf16[257,128,48]{2,1,0:T(8,128)(2,1)S(1)}, bf16[64,48,128]{2,1,0:T(8,128)(2,1)S(1)}, f32[8,128]{1,0:T(8,128)S(1)}) custom-call(s32[1]{0:T(128)} %bitcast.event_ref.refs_0_, f32[3,32768]{1,0:T(4,128)S(1)} %get-tuple-element.26.coords_ref, f32[256,128]{1,0:T(8,128)S(1)} %get-tuple-element.27.volume_ref), custom_call_target="tpu_custom_call" | custom-call | flops 4600000000 | bytes 1000000 | tf_op jit(solution)/shard_map/own_features/pallas_call | solution.py:123
  11.6 0.8 %collective-permute-done.3.second_ref = f32[2,16384]{1,0:T(2,128)S(1)} collective-permute-done((f32[2,16384]{1,0:T(2,128)S(1)}, f32[2,16384]{1,0:T(2,128)S(1)}, u32[]{:S(2)}, u32[]{:S(2)}) %collective-permute-start.3) | collective-permute-done | bytes 131104 | tf_op jit(solution)/shard_map/ppermute | solution.py:61
  12.3 0.1 collective-permute-start.4
  12.4 0.0 collective-permute-done.1.refs_0_
  12.4 0.3 collective-permute-done.2.refs_1_
  12.7 0.0 copy-done
  12.7 0.8 %halo_features.1 = (bf16[192,48,128]{2,1,0:T(8,128)(2,1)S(1)}, s32[3,8,128]{2,1,0:T(8,128)S(4)}) custom-call(s32[8,128]{1,0:T(8,128)S(1)} %get-tuple-element.25.own_ref, bf16[64,48,128]{2,1,0:T(8,128)(2,1)S(1)} %get-tuple-element.28.near_ref, s32[4,64]{1,0:T(4,128)S(1)} %bitcast.10, f32[208,128]{1,0:T(8,128)S(1)} %collective-permute-done.1.refs_0_, ...), custom_call_target="tpu_custom_call" | custom-call | flops 1150000000 | bytes 1000000 | tf_op jit(solution)/shard_map/halo_features/pallas_call | solution.py:343
  13.6 0.2 collective-permute-done.4.refs_2_
  13.7 6.5 %first_totals.1 = (f32[3,64,128]{2,1,0:T(8,128)S(1)}, f32[3,64,128]{2,1,0:T(8,128)S(1)}, f32[512,128]{1,0:T(8,128)S(1)}, bf16[257,8,256]{2,1,0:T(8,128)(2,1)S(1)}, f32[32,128,256]{2,1,0:T(8,128)S(1)}) custom-call(s32[3,8,128]{2,1,0:T(8,128)S(4)} %get-tuple-element.34.list_ref, bf16[257,128,48]{2,1,0:T(8,128)(2,1)S(1)} %get-tuple-element.35.source_ref, ...), custom_call_target="tpu_custom_call" | custom-call | flops 9200000000 | bytes 1000000 | tf_op jit(solution)/shard_map/first_totals/pallas_call | solution.py:531
  20.2 1.7 %collective-permute-start.5 = (f32[3,64,128]{2,1,0:T(8,128)S(1)}, f32[3,64,128]{2,1,0:T(8,128)S(1)}, u32[]{:S(2)}, u32[]{:S(2)}) collective-permute-start(f32[3,64,128]{2,1,0:T(8,128)S(1)} %get-tuple-element.43), channel_id=1, source_target_pairs={{0,12},{4,8},{8,4},{12,0},{1,13},{5,9},{9,5},{13,1},{2,14},{6,10},... | collective-permute-start | bytes 294920 | tf_op jit(solution)/shard_map/ppermute | solution.py:56
  21.9 0.2 collective-permute-start.6
  22.1 6.3 %last_totals.1 = (f32[3,64,128]{2,1,0:T(8,128)S(1)}, f32[32,128,256]{2,1,0:T(8,128)S(1)}) custom-call(s32[3,8,128]{2,1,0:T(8,128)S(4)} %get-tuple-element.34.list_ref, bf16[257,128,48]{2,1,0:T(8,128)(2,1)S(1)} %get-tuple-element.35.source_ref, bf16[192,48,128]{2,1,0:T(8,128)(2,1)S(1)} %get-tuple-element.36.target_ref, ...), custom_call_target="tpu_custom_call", output_to_operand_aliasing={{1}: (5, {})} | custom-call | flops 9200000000 | bytes 1000000 | tf_op jit(solution)/shard_map/last_totals/pallas_call | solution.py:566
  28.5 0.0 collective-permute-done.5.refs_1_
  28.5 0.0 collective-permute-done.6.refs_2_
  28.5 0.7 %smoothed.1 = f32[2,8192]{1,0:T(2,128)} custom-call(f32[3,64,128]{2,1,0:T(8,128)S(1)} %get-tuple-element.42.refs_0_, f32[3,64,128]{2,1,0:T(8,128)S(1)} %collective-permute-done.5.refs_1_, f32[3,64,128]{2,1,0:T(8,128)S(1)} %collective-permute-done.6.refs_2_), custom_call_target="tpu_custom_call" | custom-call | flops 230000000 | bytes 1000000 | tf_op jit(solution)/shard_map/smoothed/pallas_call | solution.py:596
  (2 shorter events, 0.1 us)
Async XLA Ops:
  0.0 2.0 %collective-permute-start = (f32[2,32768]{1,0:T(2,128)}, f32[2,32768]{1,0:T(2,128)S(1)}, u32[]{:S(2)}, u32[]{:S(2)}) collective-permute-start(f32[2,32768]{1,0:T(2,128)} %bitcast.11), channel_id=1, source_target_pairs={{1,0},{0,1},{3,2},{2,3},{5,4},{4,5},{7,6},{6,7},{9,8},{8,9},{11,10... | collective-permute-start | bytes 786440 | tf_op jit(solution)/shard_map/ppermute | solution.py:61
  2.0 10.4 %collective-permute-start.1 = (f32[208,128]{1,0:T(8,128)S(1)}, f32[208,128]{1,0:T(8,128)S(1)}, u32[]{:S(2)}, u32[]{:S(2)}) collective-permute-start(f32[208,128]{1,0:T(8,128)S(1)} %get-tuple-element.32), channel_id=1, source_target_pairs={{0,12},{4,8},{8,4},{12,0},{1,13},{5,9},{9,5},{13,1},{2,14},{6,10},... | collective-permute-start | bytes 319496 | tf_op jit(solution)/shard_map/ppermute | solution.py:56
  6.9 5.8 %collective-permute-start.2 = (f32[208,128]{1,0:T(8,128)S(1)}, f32[208,128]{1,0:T(8,128)S(1)}, u32[]{:S(2)}, u32[]{:S(2)}) collective-permute-start(f32[208,128]{1,0:T(8,128)S(1)} %get-tuple-element.33), channel_id=1, source_target_pairs={{0,4},{4,0},{8,12},{12,8},{1,5},{5,1},{9,13},{13,9},{2,6},{6,2},{1... | collective-permute-start | bytes 319496 | tf_op jit(solution)/shard_map/ppermute | solution.py:56
  6.9 5.4 %collective-permute-start.3 = (f32[2,16384]{1,0:T(2,128)S(1)}, f32[2,16384]{1,0:T(2,128)S(1)}, u32[]{:S(2)}, u32[]{:S(2)}) collective-permute-start(f32[2,16384]{1,0:T(2,128)S(1)} %get-tuple-element.37.first_ref), channel_id=1, source_target_pairs={{2,0},{3,1},{0,2},{1,3},{6,4},{7,5},{4,6},{5,7},{10,8},{11,9},{8,1... | collective-permute-start | bytes 393224 | tf_op jit(solution)/shard_map/ppermute | solution.py:61
  8.4 4.3 %copy-start = (s32[1,1,4,64]{3,2,1,0:T(4,128)S(1)}, s32[1,1,4,64]{3,2,1,0:T(4,128)}, u32[]{:S(2)}) copy-start(s32[1,1,4,64]{3,2,1,0:T(4,128)} %param.10) | copy-start | bytes 3076
  12.3 1.4 %collective-permute-start.4 = (f32[2,16384]{1,0:T(2,128)S(1)}, f32[2,16384]{1,0:T(2,128)S(1)}, u32[]{:S(2)}, u32[]{:S(2)}) collective-permute-start(f32[2,16384]{1,0:T(2,128)S(1)} %added.1.refs_1_), channel_id=1, source_target_pairs={{1,0},{0,1},{3,2},{2,3},{5,4},{4,5},{7,6},{6,7},{9,8},{8,9},{11,10... | collective-permute-start | bytes 393224 | tf_op jit(solution)/shard_map/ppermute | solution.py:61
  20.2 8.2 %collective-permute-start.5 = (f32[3,64,128]{2,1,0:T(8,128)S(1)}, f32[3,64,128]{2,1,0:T(8,128)S(1)}, u32[]{:S(2)}, u32[]{:S(2)}) collective-permute-start(f32[3,64,128]{2,1,0:T(8,128)S(1)} %get-tuple-element.43), channel_id=1, source_target_pairs={{0,12},{4,8},{8,4},{12,0},{1,13},{5,9},{9,5},{13,1},{2,14},{6,10},... | collective-permute-start | bytes 294920 | tf_op jit(solution)/shard_map/ppermute | solution.py:56
  21.9 6.5 %collective-permute-start.6 = (f32[3,64,128]{2,1,0:T(8,128)S(1)}, f32[3,64,128]{2,1,0:T(8,128)S(1)}, u32[]{:S(2)}, u32[]{:S(2)}) collective-permute-start(f32[3,64,128]{2,1,0:T(8,128)S(1)} %get-tuple-element.44), channel_id=1, source_target_pairs={{0,4},{4,0},{8,12},{12,8},{1,5},{5,1},{9,13},{13,9},{2,6},{6,2},{1... | collective-permute-start | bytes 294920 | tf_op jit(solution)/shard_map/ppermute | solution.py:56

commit v4 on v3

--- a/solution.py
+++ b/solution.py
@@ -13,7 +13,7 @@
 STEP_BITS = 5
 STEP = 1 << STEP_BITS
 SLOTS = 32
-QUOTA = 6
+QUOTA = 4
 FIELD = 10
 sigma_km = 50.0
 centre_km = 400.0

time: 29.3 us -> 29 us (0.990); the launches traced: 29.2 us -> 28.5 us
  Pallas kernels: 19 us -> 18.1 us
    pallas_call x1, Pallas kernels: 6.46 us -> 5.56 us  [first_totals(): pl.pallas_call(functools.partial(first_totals_kernel, own_blocks), out_sh...]
  transfers between devices with their start and end apart: 7 -> 7, of which waited for: 3 -> 3; matrix products, arithmetic and copies ran while one was open for 0% -> 0% of each run, Pallas kernels for 41% -> 42%
where the time goes in v4:
time: 29 us; the launch traced here: 28.5 us
  Pallas kernels  18.1 us (62%)
  starting transfers between devices  9.05 us (31%)
  waiting for transfers between devices  1.24 us (4%)
    ppermute x4, starting transfers between devices, swapped(): return lax.ppermute(block, 'cuts', route)  7.04 us
    pallas_call x1, Pallas kernels, last_totals(): pl.pallas_call(functools.partial(last_totals_kernel, own_blocks), out_sha...  6.34 us
    pallas_call x1, Pallas kernels, first_totals(): pl.pallas_call(functools.partial(first_totals_kernel, own_blocks), out_sh...  5.56 us
    pallas_call x1, Pallas kernels, own_features(): pl.pallas_call(own_features_kernel, out_shape=(pltpu.VMEM((block_total +...  3.15 us
    ppermute x3, starting transfers between devices, crossed(): return lax.ppermute(block, axis, route)  2.01 us
    pallas_call x1, Pallas kernels, prepare(): pl.pallas_call(functools.partial(prepare_kernel, strides, capacity), out_...  1.51 us
    ppermute x3, waiting for transfers between devices, crossed(): return lax.ppermute(block, axis, route)  0.95 us
    pallas_call x1, Pallas kernels, halo_features(): pl.pallas_call(functools.partial(halo_features_kernel, block_total, own_b...  0.84 us
  transfers between devices with their start and end apart: 7, of which 3 were waited for; matrix products, arithmetic and copies ran while one was open for 0% of the time, Pallas kernels for 42%

profile of v4, /device:TPU:0, one launch (start us, length us, event | category | flops | bytes accessed | tf_op | source)
XLA Modules:
  0.0 28.5 jit_solution(7581664372370124116)
XLA Ops:
  0.0 0.5 %collective-permute-start = (f32[2,32768]{1,0:T(2,128)}, f32[2,32768]{1,0:T(2,128)S(1)}, u32[]{:S(2)}, u32[]{:S(2)}) collective-permute-start(f32[2,32768]{1,0:T(2,128)} %bitcast.11), channel_id=1, source_target_pairs={{1,0},{0,1},{3,2},{2,3},{5,4},{4,5},{7,6},{6,7},{9,8},{8,9},{11,10... | collective-permute-start | bytes 786440 | tf_op jit(solution)/shard_map/ppermute | solution.py:61
  0.5 1.5 %prepare.1 = (f32[3,32768]{1,0:T(4,128)S(1)}, f32[256,128]{1,0:T(8,128)S(1)}, f32[2,16384]{1,0:T(2,128)S(1)}, s32[8,128]{1,0:T(8,128)S(1)}, f32[208,128]{1,0:T(8,128)S(1)}, /*index=5*/f32[208,128]{1,0:T(8,128)S(1)}) custom-call(s32[1]{0:T(128)} %bitcast.event_ref.refs_0_, s32[1]{0:T(128)} %bitcast.1.cut_ref, s32[1,4]{1,0:T(1,128)} %bitcast.15, ...), custom_call_target="tpu_custom_call" | custom-call | flops 2300000000 | bytes 1000000 | tf_op jit(solution)/shard_map/prepare/pallas_call | solution.py:274
  2.0 0.0 collective-permute-done.near_ref
  2.0 4.9 %collective-permute-start.1 = (f32[208,128]{1,0:T(8,128)S(1)}, f32[208,128]{1,0:T(8,128)S(1)}, u32[]{:S(2)}, u32[]{:S(2)}) collective-permute-start(f32[208,128]{1,0:T(8,128)S(1)} %get-tuple-element.32), channel_id=1, source_target_pairs={{0,12},{4,8},{8,4},{12,0},{1,13},{5,9},{9,5},{13,1},{2,14},{6,10},... | collective-permute-start | bytes 319496 | tf_op jit(solution)/shard_map/ppermute | solution.py:56
  6.9 0.0 collective-permute-start.2
  6.9 1.5 %collective-permute-start.3 = (f32[2,16384]{1,0:T(2,128)S(1)}, f32[2,16384]{1,0:T(2,128)S(1)}, u32[]{:S(2)}, u32[]{:S(2)}) collective-permute-start(f32[2,16384]{1,0:T(2,128)S(1)} %get-tuple-element.37.first_ref), channel_id=1, source_target_pairs={{2,0},{3,1},{0,2},{1,3},{6,4},{7,5},{4,6},{5,7},{10,8},{11,9},{8,1... | collective-permute-start | bytes 393224 | tf_op jit(solution)/shard_map/ppermute | solution.py:61
  8.4 0.0 copy-start
  8.4 3.2 %own_features.1 = (bf16[257,128,48]{2,1,0:T(8,128)(2,1)S(1)}, bf16[64,48,128]{2,1,0:T(8,128)(2,1)S(1)}, f32[8,128]{1,0:T(8,128)S(1)}) custom-call(s32[1]{0:T(128)} %bitcast.event_ref.refs_0_, f32[3,32768]{1,0:T(4,128)S(1)} %get-tuple-element.26.coords_ref, f32[256,128]{1,0:T(8,128)S(1)} %get-tuple-element.27.volume_ref), custom_call_target="tpu_custom_call" | custom-call | flops 4600000000 | bytes 1000000 | tf_op jit(solution)/shard_map/own_features/pallas_call | solution.py:123
  11.6 0.8 %collective-permute-done.3.second_ref = f32[2,16384]{1,0:T(2,128)S(1)} collective-permute-done((f32[2,16384]{1,0:T(2,128)S(1)}, f32[2,16384]{1,0:T(2,128)S(1)}, u32[]{:S(2)}, u32[]{:S(2)}) %collective-permute-start.3) | collective-permute-done | bytes 131104 | tf_op jit(solution)/shard_map/ppermute | solution.py:61
  12.3 0.1 collective-permute-start.4
  12.4 0.0 collective-permute-done.1.refs_0_
  12.4 0.3 collective-permute-done.2.refs_1_
  12.7 0.0 copy-done
  12.7 0.8 %halo_features.1 = (bf16[192,48,128]{2,1,0:T(8,128)(2,1)S(1)}, s32[3,8,128]{2,1,0:T(8,128)S(4)}) custom-call(s32[8,128]{1,0:T(8,128)S(1)} %get-tuple-element.25.own_ref, bf16[64,48,128]{2,1,0:T(8,128)(2,1)S(1)} %get-tuple-element.28.near_ref, s32[4,64]{1,0:T(4,128)S(1)} %bitcast.10, f32[208,128]{1,0:T(8,128)S(1)} %collective-permute-done.1.refs_0_, ...), custom_call_target="tpu_custom_call" | custom-call | flops 1150000000 | bytes 1000000 | tf_op jit(solution)/shard_map/halo_features/pallas_call | solution.py:343
  13.6 0.2 collective-permute-done.4.refs_2_
  13.7 5.6 %first_totals.1 = (f32[3,64,128]{2,1,0:T(8,128)S(1)}, f32[3,64,128]{2,1,0:T(8,128)S(1)}, f32[512,128]{1,0:T(8,128)S(1)}, bf16[257,8,256]{2,1,0:T(8,128)(2,1)S(1)}, f32[32,128,256]{2,1,0:T(8,128)S(1)}) custom-call(s32[3,8,128]{2,1,0:T(8,128)S(4)} %get-tuple-element.34.list_ref, bf16[257,128,48]{2,1,0:T(8,128)(2,1)S(1)} %get-tuple-element.35.source_ref, ...), custom_call_target="tpu_custom_call" | custom-call | flops 9200000000 | bytes 1000000 | tf_op jit(solution)/shard_map/first_totals/pallas_call | solution.py:531
  19.3 0.8 %collective-permute-start.5 = (f32[3,64,128]{2,1,0:T(8,128)S(1)}, f32[3,64,128]{2,1,0:T(8,128)S(1)}, u32[]{:S(2)}, u32[]{:S(2)}) collective-permute-start(f32[3,64,128]{2,1,0:T(8,128)S(1)} %get-tuple-element.43), channel_id=1, source_target_pairs={{0,12},{4,8},{8,4},{12,0},{1,13},{5,9},{9,5},{13,1},{2,14},{6,10},... | collective-permute-start | bytes 294920 | tf_op jit(solution)/shard_map/ppermute | solution.py:56
  20.2 1.3 %collective-permute-start.6 = (f32[3,64,128]{2,1,0:T(8,128)S(1)}, f32[3,64,128]{2,1,0:T(8,128)S(1)}, u32[]{:S(2)}, u32[]{:S(2)}) collective-permute-start(f32[3,64,128]{2,1,0:T(8,128)S(1)} %get-tuple-element.44), channel_id=1, source_target_pairs={{0,4},{4,0},{8,12},{12,8},{1,5},{5,1},{9,13},{13,9},{2,6},{6,2},{1... | collective-permute-start | bytes 294920 | tf_op jit(solution)/shard_map/ppermute | solution.py:56
  21.5 6.3 %last_totals.1 = (f32[3,64,128]{2,1,0:T(8,128)S(1)}, f32[32,128,256]{2,1,0:T(8,128)S(1)}) custom-call(s32[3,8,128]{2,1,0:T(8,128)S(4)} %get-tuple-element.34.list_ref, bf16[257,128,48]{2,1,0:T(8,128)(2,1)S(1)} %get-tuple-element.35.source_ref, bf16[192,48,128]{2,1,0:T(8,128)(2,1)S(1)} %get-tuple-element.36.target_ref, ...), custom_call_target="tpu_custom_call", output_to_operand_aliasing={{1}: (5, {})} | custom-call | flops 9200000000 | bytes 1000000 | tf_op jit(solution)/shard_map/last_totals/pallas_call | solution.py:566
  27.8 0.0 collective-permute-done.5.refs_1_
  27.8 0.0 collective-permute-done.6.refs_2_
  27.8 0.7 %smoothed.1 = f32[2,8192]{1,0:T(2,128)} custom-call(f32[3,64,128]{2,1,0:T(8,128)S(1)} %get-tuple-element.42.refs_0_, f32[3,64,128]{2,1,0:T(8,128)S(1)} %collective-permute-done.5.refs_1_, f32[3,64,128]{2,1,0:T(8,128)S(1)} %collective-permute-done.6.refs_2_), custom_call_target="tpu_custom_call" | custom-call | flops 230000000 | bytes 1000000 | tf_op jit(solution)/shard_map/smoothed/pallas_call | solution.py:596
  (2 shorter events, 0.1 us)
Async XLA Ops:
  0.0 2.0 %collective-permute-start = (f32[2,32768]{1,0:T(2,128)}, f32[2,32768]{1,0:T(2,128)S(1)}, u32[]{:S(2)}, u32[]{:S(2)}) collective-permute-start(f32[2,32768]{1,0:T(2,128)} %bitcast.11), channel_id=1, source_target_pairs={{1,0},{0,1},{3,2},{2,3},{5,4},{4,5},{7,6},{6,7},{9,8},{8,9},{11,10... | collective-permute-start | bytes 786440 | tf_op jit(solution)/shard_map/ppermute | solution.py:61
  2.0 10.4 %collective-permute-start.1 = (f32[208,128]{1,0:T(8,128)S(1)}, f32[208,128]{1,0:T(8,128)S(1)}, u32[]{:S(2)}, u32[]{:S(2)}) collective-permute-start(f32[208,128]{1,0:T(8,128)S(1)} %get-tuple-element.32), channel_id=1, source_target_pairs={{0,12},{4,8},{8,4},{12,0},{1,13},{5,9},{9,5},{13,1},{2,14},{6,10},... | collective-permute-start | bytes 319496 | tf_op jit(solution)/shard_map/ppermute | solution.py:56
  6.9 5.8 %collective-permute-start.2 = (f32[208,128]{1,0:T(8,128)S(1)}, f32[208,128]{1,0:T(8,128)S(1)}, u32[]{:S(2)}, u32[]{:S(2)}) collective-permute-start(f32[208,128]{1,0:T(8,128)S(1)} %get-tuple-element.33), channel_id=1, source_target_pairs={{0,4},{4,0},{8,12},{12,8},{1,5},{5,1},{9,13},{13,9},{2,6},{6,2},{1... | collective-permute-start | bytes 319496 | tf_op jit(solution)/shard_map/ppermute | solution.py:56
  6.9 5.4 %collective-permute-start.3 = (f32[2,16384]{1,0:T(2,128)S(1)}, f32[2,16384]{1,0:T(2,128)S(1)}, u32[]{:S(2)}, u32[]{:S(2)}) collective-permute-start(f32[2,16384]{1,0:T(2,128)S(1)} %get-tuple-element.37.first_ref), channel_id=1, source_target_pairs={{2,0},{3,1},{0,2},{1,3},{6,4},{7,5},{4,6},{5,7},{10,8},{11,9},{8,1... | collective-permute-start | bytes 393224 | tf_op jit(solution)/shard_map/ppermute | solution.py:61
  8.4 4.3 %copy-start = (s32[1,1,4,64]{3,2,1,0:T(4,128)S(1)}, s32[1,1,4,64]{3,2,1,0:T(4,128)}, u32[]{:S(2)}) copy-start(s32[1,1,4,64]{3,2,1,0:T(4,128)} %param.10) | copy-start | bytes 3076
  12.3 1.4 %collective-permute-start.4 = (f32[2,16384]{1,0:T(2,128)S(1)}, f32[2,16384]{1,0:T(2,128)S(1)}, u32[]{:S(2)}, u32[]{:S(2)}) collective-permute-start(f32[2,16384]{1,0:T(2,128)S(1)} %added.1.refs_1_), channel_id=1, source_target_pairs={{1,0},{0,1},{3,2},{2,3},{5,4},{4,5},{7,6},{6,7},{9,8},{8,9},{11,10... | collective-permute-start | bytes 393224 | tf_op jit(solution)/shard_map/ppermute | solution.py:61
  19.3 8.5 %collective-permute-start.5 = (f32[3,64,128]{2,1,0:T(8,128)S(1)}, f32[3,64,128]{2,1,0:T(8,128)S(1)}, u32[]{:S(2)}, u32[]{:S(2)}) collective-permute-start(f32[3,64,128]{2,1,0:T(8,128)S(1)} %get-tuple-element.43), channel_id=1, source_target_pairs={{0,12},{4,8},{8,4},{12,0},{1,13},{5,9},{9,5},{13,1},{2,14},{6,10},... | collective-permute-start | bytes 294920 | tf_op jit(solution)/shard_map/ppermute | solution.py:56
  20.2 7.7 %collective-permute-start.6 = (f32[3,64,128]{2,1,0:T(8,128)S(1)}, f32[3,64,128]{2,1,0:T(8,128)S(1)}, u32[]{:S(2)}, u32[]{:S(2)}) collective-permute-start(f32[3,64,128]{2,1,0:T(8,128)S(1)} %get-tuple-element.44), channel_id=1, source_target_pairs={{0,4},{4,0},{8,12},{12,8},{1,5},{5,1},{9,13},{13,9},{2,6},{6,2},{1... | collective-permute-start | bytes 294920 | tf_op jit(solution)/shard_map/ppermute | solution.py:56
